TPU v7x, 256 devices: a whole 4x4x8 slice. The times are simulated.
256 devices in a mesh: cols: 32 (over y, x, core), rows: 8 (over z).
Axes of the slice: x: 4, y: 4, z: 8, core: 2. Of those that a mesh axis runs over, the one named last changes fastest.
Arguments:
- latent: bfloat16 [64, 2048, 256], P('rows', 'cols'), may hold values from -6 to 6
- cotangent: bfloat16 [128, 4096, 256], P('rows', 'cols'), may hold values from -12 to 12
- pixel_mask: int32 [128, 4096], P('rows', 'cols'), may hold values 0 or 1
- res_kernels: bfloat16 [6, 3, 3, 256, 256], replicated, may hold values from -0.125 to 0.125
- up_kernel: bfloat16 [3, 3, 256, 256], replicated, may hold values from -0.125 to 0.125
Outputs:
- latent_grad: float32 [64, 2048, 256], P('rows', 'cols')
All inputs are finite; a program needn't handle non-finite values. No bound on the sum of `pixel_mask` on one device may be relied on, other than what follows from the above.
Results may differ from a plain program's by a relative error of at most 0.014.
Values may be sent and summed in bfloat16 or wider, within the bound.
A program may use at most 128 MiB of HBM per device.

v0:
```python
import jax
import jax.numpy as jnp
from jax import lax
from jax.sharding import PartitionSpec as P

GROUPS = 32
LAYERS = 3


EPS = 1e-06


def padded_2(block, sides, width):
    for axis, dim in sides:
        count = lax.axis_size(axis)
        forward = [(i, i + 1) for i in range(count - 1)]
        backward = [(target, source) for source, target in forward]
        low = lax.ppermute(
            lax.slice_in_dim(block, block.shape[dim] - width, None, axis=dim), axis, forward
        )
        high = lax.ppermute(lax.slice_in_dim(block, 0, width, axis=dim), axis, backward)
        block = jnp.concatenate([low, block, high], axis=dim)
    return block


def tile_conv(padded, kernel):
    return lax.conv_general_dilated(
        padded[None],
        kernel,
        (1, 1),
        "VALID",
        dimension_numbers=("NHWC", "HWIO", "NHWC"),
        preferred_element_type=jnp.float32,
    )[0]


def flipped(kernel):
    return jnp.transpose(kernel[::-1, ::-1], (0, 1, 3, 2))


def forward_conv(active, kernel):
    padded = padded_2(active, (("cols", 1), ("rows", 0)), 1)
    return tile_conv(padded, kernel)


def backward_conv(gradient, kernel):
    padded = padded_2(gradient.astype(jnp.bfloat16), (("cols", 1), ("rows", 0)), 1)
    return tile_conv(padded, flipped(kernel))


def silu_slope(tensor):
    logistic = jax.nn.sigmoid(tensor)
    return logistic * (1.0 + tensor * (1.0 - logistic))


def members(grouped):
    return grouped.shape[0] * grouped.shape[2] * lax.axis_size("cols") * lax.axis_size("rows")


def norm_forward(tensor):
    grouped = tensor.reshape(-1, GROUPS, tensor.shape[-1] // GROUPS)
    number = members(grouped)
    average = lax.psum(jnp.sum(grouped, axis=(0, 2)), ("cols", "rows")) / number
    centred = grouped - average[None, :, None]
    spread = lax.psum(jnp.sum(centred * centred, axis=(0, 2)), ("cols", "rows")) / number
    inverse = lax.rsqrt(spread + EPS)
    return ((centred * inverse[None, :, None]).reshape(tensor.shape), inverse)


def norm_backward(gradient, normed, inverse):
    grouped = gradient.reshape(-1, GROUPS, gradient.shape[-1] // GROUPS)
    normal_g = normed.reshape(grouped.shape)
    number = members(grouped)
    total_grad, cross_grad = lax.psum(
        (jnp.sum(grouped, axis=(0, 2)), jnp.sum(grouped * normal_g, axis=(0, 2))), ("cols", "rows")
    )
    result = inverse[None, :, None] * (
        grouped
        - (total_grad / number)[None, :, None]
        - normal_g * (cross_grad / number)[None, :, None]
    )
    return result.reshape(gradient.shape)


def per_device(latent, cotangent, pixel_mask, res_kernels, up_kernel):
    stream = latent.astype(jnp.float32)
    stored = []
    for layer_index in range(LAYERS):
        first_norm, first_inv = norm_forward(stream)
        hidden = forward_conv(
            jax.nn.silu(first_norm).astype(jnp.bfloat16), res_kernels[2 * layer_index]
        )
        second_norm, second_inv = norm_forward(hidden)
        stored.append((first_norm, first_inv, second_norm, second_inv))
        if layer_index + 1 < LAYERS:
            stream = stream + forward_conv(
                jax.nn.silu(second_norm).astype(jnp.bfloat16), res_kernels[2 * layer_index + 1]
            )
    masked = (pixel_mask.astype(jnp.float32)[:, :, None] * cotangent.astype(jnp.float32)).astype(
        jnp.bfloat16
    )
    tile_rows = latent.shape[0]
    tile_cols = latent.shape[1]
    padded = padded_2(masked, (("cols", 1), ("rows", 0)), 1)
    upsampled = tile_conv(padded, flipped(up_kernel))
    gradient = upsampled.reshape(tile_rows, 2, tile_cols, 2, upsampled.shape[-1]).sum(axis=(1, 3))
    for layer_index in reversed(range(LAYERS)):
        first_norm, first_inv, second_norm, second_inv = stored[layer_index]
        second_grad = backward_conv(gradient, res_kernels[2 * layer_index + 1]) * silu_slope(
            second_norm
        )
        hidden_grad = norm_backward(second_grad, second_norm, second_inv)
        first_grad = backward_conv(hidden_grad, res_kernels[2 * layer_index]) * silu_slope(
            first_norm
        )
        gradient = gradient + norm_backward(first_grad, first_norm, first_inv)
    return gradient


def solution(mesh):
    in_specs = (P("rows", "cols", None), P("rows", "cols", None), P("rows", "cols"), P(), P())
    out_specs = P("rows", "cols", None)
    return jax.shard_map(
        per_device, mesh=mesh, in_specs=in_specs, out_specs=out_specs, check_vma=False
    )
```

profile of v0, /device:TPU:1, one launch (start us, length us, event | category | flops | bytes accessed | tf_op | source)
XLA Modules:
  0.0 1638.6 jit_solution(7183606705890567883)
XLA Ops:
  1.4 81.4 %psum.168 = f32[32]{0:T(128)S(1)} all-reduce(f32[32]{0:T(128)S(1)} %reduce_sum.293), channel_id=1, replica_groups=mesh['cols'=32,'rows'=8] {'cols','rows'}, use_global_device_ids=true, to_apply=%region_3.0 | all-reduce | flops 32 | bytes 256 | tf_op jit(solution)/shard_map/psum | solution.py:63
  84.3 72.4 %psum.169 = f32[32]{0:T(128)S(1)} all-reduce(f32[32]{0:T(128)S(1)} %reduce_sum.299), channel_id=1, replica_groups=mesh['cols'=32,'rows'=8] {'cols','rows'}, use_global_device_ids=true, to_apply=%region_6.7 | all-reduce | flops 32 | bytes 256 | tf_op jit(solution)/shard_map/psum | solution.py:65
  158.1 2.8 collective-permute-start.4
  162.9 3.0 collective-permute-done.5
  166.0 3.7 collective-permute-start.6
  171.0 3.7 collective-permute-done.7
  178.1 76.5 %psum.170 = f32[32]{0:T(128)S(1)} all-reduce(f32[32]{0:T(128)S(1)} %reduce_sum.302), channel_id=1, replica_groups=mesh['cols'=32,'rows'=8] {'cols','rows'}, use_global_device_ids=true, to_apply=%region_9.10 | all-reduce | flops 32 | bytes 256 | tf_op jit(solution)/shard_map/psum | solution.py:63
  255.4 73.6 %psum.171 = f32[32]{0:T(128)S(1)} all-reduce(f32[32]{0:T(128)S(1)} %reduce_sum.308), channel_id=1, replica_groups=mesh['cols'=32,'rows'=8] {'cols','rows'}, use_global_device_ids=true, to_apply=%region_12.13 | all-reduce | flops 32 | bytes 256 | tf_op jit(solution)/shard_map/psum | solution.py:65
  329.3 3.5 collective-permute-start.8
  337.9 3.7 collective-permute-start.10
  342.9 3.7 collective-permute-done.11
  350.7 3.7 collective-permute-start
  354.4 76.5 %psum.172 = f32[32]{0:T(128)S(1)} all-reduce(f32[32]{0:T(128)S(1)} %reduce_sum.314), channel_id=1, replica_groups=mesh['cols'=32,'rows'=8] {'cols','rows'}, use_global_device_ids=true, to_apply=%region_15.16 | all-reduce | flops 32 | bytes 256 | tf_op jit(solution)/shard_map/psum | solution.py:63
  431.4 2.6 collective-permute-start.1
  434.0 73.9 %psum.173 = f32[32]{0:T(128)S(1)} all-reduce(f32[32]{0:T(128)S(1)} %reduce_sum.317), channel_id=1, replica_groups=mesh['cols'=32,'rows'=8] {'cols','rows'}, use_global_device_ids=true, to_apply=%region_18.19 | all-reduce | flops 32 | bytes 256 | tf_op jit(solution)/shard_map/psum | solution.py:65
  508.7 3.3 collective-permute-start.12
  513.9 3.7 collective-permute-start.2
  519.7 4.6 collective-permute-start.14
  528.0 2.8 copy.7
  536.1 77.9 %psum.174 = f32[32]{0:T(128)S(1)} all-reduce(f32[32]{0:T(128)S(1)} %reduce_sum.323), channel_id=1, replica_groups=mesh['cols'=32,'rows'=8] {'cols','rows'}, use_global_device_ids=true, to_apply=%region_21.22 | all-reduce | flops 32 | bytes 256 | tf_op jit(solution)/shard_map/psum | solution.py:63
  614.8 73.9 %psum.175 = f32[32]{0:T(128)S(1)} all-reduce(f32[32]{0:T(128)S(1)} %reduce_sum.329), channel_id=1, replica_groups=mesh['cols'=32,'rows'=8] {'cols','rows'}, use_global_device_ids=true, to_apply=%region_24.25 | all-reduce | flops 32 | bytes 256 | tf_op jit(solution)/shard_map/psum | solution.py:65
  689.1 2.8 collective-permute-start.16
  693.9 4.3 convolution_select_fusion
  700.5 3.5 reshape_squeeze.12
  704.0 3.2 reduce_sum.287
  710.9 3.9 collective-permute-done.19
  718.1 4.7 collective-permute-start.24
  722.7 78.5 %psum.176 = f32[32]{0:T(128)S(1)} all-reduce(f32[32]{0:T(128)S(1)} %reduce_sum.332), channel_id=1, replica_groups=mesh['cols'=32,'rows'=8] {'cols','rows'}, use_global_device_ids=true, to_apply=%region_27.28 | all-reduce | flops 32 | bytes 256 | tf_op jit(solution)/shard_map/psum | solution.py:63
  801.7 2.6 collective-permute-start.25
  804.3 73.7 %psum.177 = f32[32]{0:T(128)S(1)} all-reduce(f32[32]{0:T(128)S(1)} %reduce_sum.338), channel_id=1, replica_groups=mesh['cols'=32,'rows'=8] {'cols','rows'}, use_global_device_ids=true, to_apply=%region_30.31 | all-reduce | flops 32 | bytes 256 | tf_op jit(solution)/shard_map/psum | solution.py:65
  878.3 3.3 collective-permute-start.20
  883.7 3.7 collective-permute-start.26
  888.8 4.0 collective-permute-start.22
  895.3 3.1 collective-permute-done.23
  899.0 2.9 select_reduce_fusion.7
  903.3 79.3 %psum.178 = f32[32]{0:T(128)S(1)} all-reduce(f32[32]{0:T(128)S(1)} %reduce_sum.344), channel_id=1, replica_groups=mesh['cols'=32,'rows'=8] {'cols','rows'}, use_global_device_ids=true, to_apply=%region_33.34 | all-reduce | flops 32 | bytes 256 | tf_op jit(solution)/shard_map/psum | solution.py:63
  984.2 72.3 %psum.179 = f32[32]{0:T(128)S(1)} all-reduce(f32[32]{0:T(128)S(1)} %reduce_sum.347), channel_id=1, replica_groups=mesh['cols'=32,'rows'=8] {'cols','rows'}, use_global_device_ids=true, to_apply=%region_36.37 | all-reduce | flops 32 | bytes 256 | tf_op jit(solution)/shard_map/psum | solution.py:65
  1056.7 3.2 select_reduce_fusion.5
  1062.5 73.7 %all-reduce.5 = (f32[32]{0:T(128)S(1)}, f32[32]{0:T(128)S(1)}) all-reduce(f32[32]{0:T(128)S(1)} %reduce_sum.359, f32[32]{0:T(128)S(1)} %reduce_sum.353), channel_id=1, replica_groups=mesh['cols'=32,'rows'=8] {'cols','rows'}, use_global_device_ids=true, to_apply=%region_42.43 | all-reduce | flops 64 | bytes 512 | tf_op jit(solution)/shard_map/psum | solution.py:74
  1138.1 3.4 collective-permute-start.28
  1143.4 3.0 collective-permute-done.29
  1146.5 2.8 collective-permute-start.30
  1151.0 3.3 collective-permute-done.31
  1158.8 77.5 %all-reduce.4 = (f32[32]{0:T(128)S(1)}, f32[32]{0:T(128)S(1)}) all-reduce(f32[32]{0:T(128)S(1)} %reduce_sum.441, f32[32]{0:T(128)S(1)} %reduce_sum.362), channel_id=1, replica_groups=mesh['cols'=32,'rows'=8] {'cols','rows'}, use_global_device_ids=true, to_apply=%region_48.49 | all-reduce | flops 64 | bytes 512 | tf_op jit(solution)/shard_map/psum | solution.py:74
  1238.7 3.8 collective-permute-start.32
  1244.5 3.0 collective-permute-done.33
  1250.5 3.7 collective-permute-done.35
  1255.6 2.3 select_reduce_fusion.3
  1258.3 78.6 %all-reduce.3 = (f32[32]{0:T(128)S(1)}, f32[32]{0:T(128)S(1)}) all-reduce(f32[32]{0:T(128)S(1)} %reduce_sum.447, f32[32]{0:T(128)S(1)} %reduce_sum.444), channel_id=1, replica_groups=mesh['cols'=32,'rows'=8] {'cols','rows'}, use_global_device_ids=true, to_apply=%region_54.55 | all-reduce | flops 64 | bytes 512 | tf_op jit(solution)/shard_map/psum | solution.py:74
  1337.8 3.8 collective-permute-start.36
  1343.5 3.0 collective-permute-done.37
  1349.2 3.7 collective-permute-done.39
  1353.5 2.2 convolution_select_fusion.3
  1357.0 78.9 %all-reduce.2 = (f32[32]{0:T(128)S(1)}, f32[32]{0:T(128)S(1)}) all-reduce(f32[32]{0:T(128)S(1)} %reduce_sum.453, f32[32]{0:T(128)S(1)} %reduce_sum.450), channel_id=1, replica_groups=mesh['cols'=32,'rows'=8] {'cols','rows'}, use_global_device_ids=true, to_apply=%region_60.61 | all-reduce | flops 64 | bytes 512 | tf_op jit(solution)/shard_map/psum | solution.py:74
  1437.6 3.8 collective-permute-start.40
  1443.4 3.0 collective-permute-done.41
  1449.2 3.5 collective-permute-done.43
  1454.2 3.1 select_reduce_fusion.1
  1457.7 78.9 %all-reduce.1 = (f32[32]{0:T(128)S(1)}, f32[32]{0:T(128)S(1)}) all-reduce(f32[32]{0:T(128)S(1)} %reduce_sum.459, f32[32]{0:T(128)S(1)} %reduce_sum.456), channel_id=1, replica_groups=mesh['cols'=32,'rows'=8] {'cols','rows'}, use_global_device_ids=true, to_apply=%region_66.67 | all-reduce | flops 64 | bytes 512 | tf_op jit(solution)/shard_map/psum | solution.py:74
  1538.5 3.8 collective-permute-start.44
  1544.3 3.0 collective-permute-done.45
  1550.0 3.7 collective-permute-done.47
  1554.3 2.2 convolution_select_fusion.1
  1557.9 79.0 %all-reduce = (f32[32]{0:T(128)S(1)}, f32[32]{0:T(128)S(1)}) all-reduce(f32[32]{0:T(128)S(1)} %reduce_sum.465, f32[32]{0:T(128)S(1)} %reduce_sum.462), channel_id=1, replica_groups=mesh['cols'=32,'rows'=8] {'cols','rows'}, use_global_device_ids=true, to_apply=%region_72.73 | all-reduce | flops 64 | bytes 512 | tf_op jit(solution)/shard_map/psum | solution.py:74
  (356 shorter events, 106.0 us)
Async XLA Ops:
  0.0 693.9 %copy-start = (bf16[3,3,256,256]{3,2,1,0:T(8,128)(2,1)S(1)}, bf16[3,3,256,256]{3,2,1,0:T(8,128)(2,1)}, u32[]{:S(2)}) copy-start(bf16[3,3,256,256]{3,2,1,0:T(8,128)(2,1)} %param.9) | copy-start | bytes 3538948
  156.9 18.2 %copy-start.16 = (f32[256]{0:T(256)}, f32[256]{0:T(256)S(1)}, u32[]{:S(2)}) copy-start(f32[256]{0:T(256)S(1)} %mul.418) | copy-start | bytes 3076
  158.1 4.8 collective-permute-start.4
  161.0 4.9 collective-permute-start.5
  166.0 5.0 collective-permute-start.6
  169.7 5.0 collective-permute-start.7
  177.9 151.4 %copy-start.7 = (f32[8,8,9,256]{3,1,2,0:T(8,128)}, f32[8,8,9,256]{3,1,2,0:T(8,128)S(1)}, u32[]{:S(2)}) copy-start(f32[8,8,9,256]{3,1,2,0:T(8,128)S(1)} %get-tuple-element.87) | copy-start | bytes 1769476
  254.8 74.5 %copy-start.18 = (f32[256]{0:T(256)}, f32[256]{0:T(256)S(1)}, u32[]{:S(2)}) copy-start(f32[256]{0:T(256)S(1)} %sub.263) | copy-start | bytes 3076
  255.4 77.5 %copy-start.2 = (f32[8,8,9,256]{3,0,2,1:T(8,128)}, f32[8,8,9,256]{3,0,2,1:T(8,128)S(1)}, u32[]{:S(2)}) copy-start(f32[8,8,9,256]{3,0,2,1:T(8,128)S(1)} %copy.13) | copy-start | bytes 1769476
  329.1 3.7 copy-start.26
  329.3 7.0 collective-permute-start.8
  332.9 4.9 collective-permute-start.9
  337.9 5.0 collective-permute-start.10
  341.6 5.0 collective-permute-start.11
  350.7 163.2 %collective-permute-start = (bf16[16,1,256]{2,1,0:T(2,128)(2,1)S(1)}, bf16[16,1,256]{2,1,0:T(2,128)(2,1)S(1)}, u32[]{:S(2)}, u32[]{:S(2)}) collective-permute-start(bf16[16,1,256]{2,1,0:T(2,128)(2,1)S(1)} %get-tuple-element.40), channel_id=1, source_target_pairs={{0,8},{8,16},{16,24},{24,32},{32,40},{40,48},{48,56},{56,64},{64,7... | collective-permute-start | bytes 24584 | tf_op jit(solution)/shard_map/ppermute | solution.py:18
  431.1 82.8 %copy-start.12 = (f32[256]{0:T(256)}, f32[256]{0:T(256)S(1)}, u32[]{:S(2)}) copy-start(f32[256]{0:T(256)S(1)} %sub.269) | copy-start | bytes 3076
  431.4 82.5 %collective-permute-start.1 = (bf16[16,1,256]{2,1,0:T(2,128)(2,1)S(1)}, bf16[16,1,256]{2,1,0:T(2,128)(2,1)S(1)}, u32[]{:S(2)}, u32[]{:S(2)}) collective-permute-start(bf16[16,1,256]{2,1,0:T(2,128)(2,1)S(1)} %get-tuple-element.41), channel_id=1, source_target_pairs={{8,0},{16,8},{24,16},{32,24},{40,32},{48,40},{56,48},{64,56},{72,6... | collective-permute-start | bytes 24584 | tf_op jit(solution)/shard_map/ppermute | solution.py:21
  508.7 10.3 collective-permute-start.12
  511.9 7.0 collective-permute-start.13
  513.9 11.8 collective-permute-start.2
  517.6 8.2 collective-permute-start.3
  518.9 6.9 copy-start.20
  519.0 6.8 copy-start.22
  519.7 11.2 collective-permute-start.14
  524.3 6.6 collective-permute-start.15
  528.0 2.8 copy-start.21
  528.0 2.8 copy-start.23
  535.0 79.9 %copy-start.9 = (f32[8,8,9,256]{3,1,2,0:T(8,128)}, f32[8,8,9,256]{3,1,2,0:T(8,128)S(1)}, u32[]{:S(2)}) copy-start(f32[8,8,9,256]{3,1,2,0:T(8,128)S(1)} %get-tuple-element.89) | copy-start | bytes 1769476
  614.4 79.5 %copy-start.29 = (pred[8,17]{0,1:T(8,128)(4,1)S(1)}, pred[8,17]{0,1:T(8,128)(4,1)}, u32[]{:S(2)}) copy-start(pred[8,17]{0,1:T(8,128)(4,1)} %constant.98) | copy-start | bytes 412
  614.8 83.4 %copy-start.4 = (f32[8,8,9,256]{3,0,2,1:T(8,128)}, f32[8,8,9,256]{3,0,2,1:T(8,128)S(1)}, u32[]{:S(2)}) copy-start(f32[8,8,9,256]{3,0,2,1:T(8,128)S(1)} %copy.21) | copy-start | bytes 1769476
  689.1 18.1 %collective-permute-start.16 = (bf16[8,1,256]{2,0,1:T(8,128)(2,1)S(1)}, bf16[8,1,256]{2,0,1:T(8,128)(2,1)S(1)}, u32[]{:S(2)}, u32[]{:S(2)}) collective-permute-start(bf16[8,1,256]{2,0,1:T(8,128)(2,1)S(1)} %get-tuple-element.78), channel_id=1, source_target_pairs={{0,8},{8,16},{16,24},{24,32},{32,40},{40,48},{48,56},{56,64},{64,7... | collective-permute-start | bytes 12296 | tf_op jit(solution)/shard_map/ppermute | solution.py:18
  692.0 15.3 collective-permute-start.17
  707.4 3.6 collective-permute-start.18
  709.4 5.5 collective-permute-start.19
  718.1 165.5 %collective-permute-start.24 = (bf16[8,1,256]{2,0,1:T(8,128)(2,1)S(1)}, bf16[8,1,256]{2,0,1:T(8,128)(2,1)S(1)}, u32[]{:S(2)}, u32[]{:S(2)}) collective-permute-start(bf16[8,1,256]{2,0,1:T(8,128)(2,1)S(1)} %get-tuple-element.76), channel_id=1, source_target_pairs={{0,8},{8,16},{16,24},{24,32},{32,40},{40,48},{48,56},{56,64},{64,7... | collective-permute-start | bytes 12296 | tf_op jit(solution)/shard_map/ppermute | solution.py:18
  801.7 81.8 %collective-permute-start.25 = (bf16[8,1,256]{2,0,1:T(8,128)(2,1)S(1)}, bf16[8,1,256]{2,0,1:T(8,128)(2,1)S(1)}, u32[]{:S(2)}, u32[]{:S(2)}) collective-permute-start(bf16[8,1,256]{2,0,1:T(8,128)(2,1)S(1)} %get-tuple-element.77), channel_id=1, source_target_pairs={{8,0},{16,8},{24,16},{32,24},{40,32},{48,40},{56,48},{64,56},{72,6... | collective-permute-start | bytes 12296 | tf_op jit(solution)/shard_map/ppermute | solution.py:21
  878.3 10.3 collective-permute-start.20
  881.6 7.1 collective-permute-start.21
  883.7 10.4 collective-permute-start.26
  887.4 6.7 collective-permute-start.27
  888.8 6.5 collective-permute-start.22
  892.8 5.7 collective-permute-start.23
  1138.1 5.3 collective-permute-start.28
  1141.5 4.9 collective-permute-start.29
  1146.5 4.5 collective-permute-start.30
  1149.3 5.0 collective-permute-start.31
  1238.7 5.7 collective-permute-start.32
  1242.5 4.9 collective-permute-start.33
  1247.5 2.9 collective-permute-start.34
  1249.2 5.0 collective-permute-start.35
  1257.9 79.5 %copy-start.5 = (f32[8,8,9,256]{3,0,2,1:T(8,128)S(1)}, f32[8,8,9,256]{3,0,2,1:T(8,128)}, u32[]{:S(2)}) copy-start(f32[8,8,9,256]{3,0,2,1:T(8,128)} %copy-done.4) | copy-start | bytes 1769476
  1337.8 5.8 collective-permute-start.36
  1341.6 4.9 collective-permute-start.37
  1346.6 2.6 collective-permute-start.38
  1347.9 5.0 collective-permute-start.39
  1437.6 5.8 collective-permute-start.40
  1441.4 4.9 collective-permute-start.41
  1446.5 2.8 collective-permute-start.42
  1447.8 5.0 collective-permute-start.43
  1457.3 80.9 %copy-start.3 = (f32[8,8,9,256]{3,0,2,1:T(8,128)S(1)}, f32[8,8,9,256]{3,0,2,1:T(8,128)}, u32[]{:S(2)}) copy-start(f32[8,8,9,256]{3,0,2,1:T(8,128)} %copy-done.2) | copy-start | bytes 1769476
  1538.5 5.8 collective-permute-start.44
  1542.4 4.9 collective-permute-start.45
  1547.4 2.6 collective-permute-start.46
  1548.7 5.0 collective-permute-start.47
  (14 other events, 13.6 us)
where the time goes:
time: 1650 us; the launch traced here: 1640 us
  blocking collectives  1380 us (84%)
  starting transfers between devices  117 us (7%)
  waiting for transfers between devices  51.9 us (3%)
  local copies, waits for them, and re-layouts  33.6 us (2%)
  matrix products  31 us (2%)
  other arithmetic  26.4 us (2%)
    psum x6, blocking collectives, norm_forward(): average = lax.psum(jnp.sum(grouped, axis=(0, 2)), ('cols', 'rows')) / number  470 us
    psum x6, blocking collectives, norm_backward(): lax.psum((jnp.sum(grouped, axis=(0, 2)), jnp.sum(grouped * normal_g, axis...  467 us
    psum x6, blocking collectives, norm_forward(): lax.psum(jnp.sum(centred * centred, axis=(0, 2)), ('cols', 'rows')) / number  440 us
    ppermute x24, starting transfers between devices, padded_2(): lax.ppermute(lax.slice_in_dim(block, block.shape[dim] - width, None, axis...  76.3 us
    ppermute x24, waiting for transfers between devices, padded_2(): lax.ppermute(lax.slice_in_dim(block, 0, width, axis=dim), axis, backward)  51.7 us
    ppermute x24, starting transfers between devices, padded_2(): lax.ppermute(lax.slice_in_dim(block, 0, width, axis=dim), axis, backward)  40.8 us
  transfers between devices with their start and end apart: 48, of which 16 were waited for; matrix products, arithmetic and copies ran while one was open for 1% of the time, Pallas kernels for 0%

commit v1 on v0

v1 whole, which is shorter than its diff:
```python
import functools

import jax
import jax.numpy as jnp
from jax import lax
from jax.experimental import pallas as pl
from jax.experimental.pallas import tpu as pltpu
from jax.sharding import PartitionSpec as P

LAYERS = 3
EPS = 1e-06
MESH = pl.DeviceIdType.MESH
F32 = jnp.float32
BF16 = jnp.bfloat16

H, W, C = 8, 64, 256
WT = W + 8
FH, FW = 2 * H, 2 * W
FWT = FW + 16
SIDE = 16
PIXELS = H * W
GROUP = 8


def position():
    c = lax.axis_index("cols")
    r = lax.axis_index("rows")
    core = c % 2
    chip = c // 2
    return c, r, core, chip % 4, chip // 4


def plane_peers():
    c, r, core, x, y = position()
    out = []
    for dy in range(4):
        for dx in range(4):
            if dx or dy:
                far = min(dx, 4 - dx) + min(dy, 4 - dy)
                out.append((far, dy * 4 + dx, (((y + dy) % 4) * 4 + (x + dx) % 4) * 2 + core, r))
    return [p[1:] for p in sorted(out, key=lambda p: -p[0])]


def column_peers():
    c, r, core, x, y = position()
    out = []
    for dz in range(8):
        for dc in range(2):
            if dz or dc:
                far = min(dz, 8 - dz)
                out.append((far, dz * 2 + dc, c - core + (core + dc) % 2, (r + dz) % 8))
    return [p[1:] for p in sorted(out, key=lambda p: -p[0])]


def neighbours():
    c, r, core, x, y = position()
    out = []
    for dr in (-1, 0, 1):
        for dc in (-1, 0, 1):
            if dr or dc:
                out.append((dr, dc, (c + dc + 32) % 32, (r + dr + 8) % 8))
    return out


def halo_copies(field, height, width, total, send, recv):
    copies = []
    for i, (dr, dc, col, row) in enumerate(neighbours()):
        src_r = pl.ds(1, height) if dr == 0 else (pl.ds(1, 1) if dr < 0 else pl.ds(height, 1))
        dst_r = pl.ds(1, height) if dr == 0 else (pl.ds(height + 1, 1) if dr < 0 else pl.ds(0, 1))
        src_c = pl.ds(0, width) if dc == 0 else (pl.ds(0, 1) if dc < 0 else pl.ds(width - 1, 1))
        dst_c = pl.ds(0, width) if dc == 0 else (pl.ds(width, 1) if dc < 0 else pl.ds(total - 1, 1))
        src, dst = (src_r, src_c, slice(None)), (dst_r, dst_c, slice(None))
        if len(field.shape) == 4:
            src, dst = (slice(None),) + src, (slice(None),) + dst
        copies.append(
            pltpu.make_async_remote_copy(
                src_ref=field.at[src],
                dst_ref=field.at[dst],
                send_sem=send.at[i],
                recv_sem=recv.at[i],
                device_id={"cols": col, "rows": row},
                device_id_type=MESH,
            )
        )
    return copies


def phase_start(buf, peers, send, recv):
    for slot, col, row in peers:
        pltpu.make_async_remote_copy(
            src_ref=buf.at[0],
            dst_ref=buf.at[slot],
            send_sem=send,
            recv_sem=recv,
            device_id={"cols": col, "rows": row},
            device_id_type=MESH,
        ).start()


def phase_wait(buf, sem):
    pltpu.make_async_copy(buf.at[pl.ds(1, SIDE - 1)], buf.at[pl.ds(1, SIDE - 1)], sem).wait()


def merge_moments(parts, count):
    mean = jnp.sum(parts[:, 0:2], axis=0) * (1.0 / SIDE)
    delta = parts[:, 0:2] - mean[None]
    square = jnp.sum(parts[:, 2:4] + delta * delta * float(count), axis=0)
    return mean, square


def lane_swap(value, step):
    lane = lax.broadcasted_iota(jnp.int32, value.shape, 1)
    return jnp.where((lane & step) != 0, pltpu.roll(value, step, 1), pltpu.roll(value, 128 - step, 1))


def wide(value):
    return jnp.concatenate([value[0:1], value[1:2]], axis=1).reshape(1, 1, C)


def sigmoid(v):
    return 1.0 / (1.0 + jnp.exp(-v))


def kernel(
    latent, mask, cot_hbm, res_hbm, up_hbm, out,
    cot, weights, fields, grads, total, fine, slopes, stats, taps, box_a, box_b, buf_a, buf_b,
    load_sem, send_a, send_b, recv_a, recv_b, hsend, hrecv,
):
    c, r, _, _, _ = position()
    top = jnp.where(r == 0, 0.0, 1.0).astype(F32)
    bottom = jnp.where(r == 7, 0.0, 1.0).astype(F32)
    left = jnp.where(c == 0, 0.0, 1.0).astype(F32)
    right = jnp.where(c == 31, 0.0, 1.0).astype(F32)
    side = lax.broadcasted_iota(jnp.int32, (1, 8, C), 1)
    edge = jnp.where(side == 0, right, jnp.where(side == 7, left, 0.0))

    barrier = pltpu.get_barrier_semaphore()
    plane, column = plane_peers(), column_peers()
    greeted = [p[1:] for p in plane] + [p[1:] for p in column] + [p[2:] for p in neighbours()]
    for col, row in greeted:
        pl.semaphore_signal(barrier, inc=1, device_id={"cols": col, "rows": row}, device_id_type=MESH)

    def weight_copy(k):
        return pltpu.make_async_copy(res_hbm.at[k], weights.at[k], load_sem.at[k])

    up_copy = pltpu.make_async_copy(up_hbm, weights.at[6], load_sem.at[6])
    cot_copy = pltpu.make_async_copy(cot_hbm, cot, load_sem.at[7])
    cot_copy.start()
    weight_copy(0).start()
    up_copy.start()
    for k in range(1, 6):
        weight_copy(k).start()

    def load_stats(k):
        return stats[k, 0:1, :].reshape(1, 1, C), stats[k, 1:2, :].reshape(1, 1, C)

    def put_moments(k, x):
        mean = jnp.sum(x, axis=(0, 1)).reshape(1, C) * (1.0 / PIXELS)
        delta = x - mean.reshape(1, 1, C)
        square = jnp.sum(delta * delta, axis=(0, 1)).reshape(1, C)
        buf_a[k, 0, 0:1, :] = mean[:, 0:128]
        buf_a[k, 0, 1:2, :] = mean[:, 128:256]
        buf_a[k, 0, 2:3, :] = square[:, 0:128]
        buf_a[k, 0, 3:4, :] = square[:, 128:256]

    def put_sums(t, d, normed):
        first = jnp.sum(d, axis=(0, 1)).reshape(1, C) * (1.0 / PIXELS)
        second = jnp.sum(d * normed, axis=(0, 1)).reshape(1, C) * (1.0 / PIXELS)
        buf_a[t, 0, 0:1, :] = first[:, 0:128]
        buf_a[t, 0, 1:2, :] = first[:, 128:256]
        buf_a[t, 0, 2:3, :] = second[:, 0:128]
        buf_a[t, 0, 3:4, :] = second[:, 128:256]

    def start_a(t):
        phase_start(buf_a.at[t], plane, send_a.at[t], recv_a.at[t])

    def start_b(t):
        phase_start(buf_b.at[t], column, send_b.at[t], recv_b.at[t])

    def field_copies(k):
        return halo_copies(fields.at[k], H, W, WT, hsend.at[k], hrecv.at[k])

    def grad_copies(k):
        return halo_copies(grads.at[k], H, W, WT, hsend.at[k + 6], hrecv.at[k + 6])

    def total_copies():
        return halo_copies(total, H, W, WT, hsend.at[12], hrecv.at[12])

    def fine_copies():
        return halo_copies(fine, FH, FW, FWT, hsend.at[13], hrecv.at[13])

    def put_taps(make):
        for first, rows, scale in ((0, 1, top), (1, H, None), (H + 1, 1, bottom)):
            u = make(first, rows)
            if scale is not None:
                u = u * scale
            u = jnp.concatenate([u[:, 0:W], u[:, W:WT] * edge], axis=1)
            at = slice(first, first + rows)
            taps[at, :, 0:C] = pltpu.roll(u, 1, 1)[:, 0:W].astype(BF16)
            taps[at, :, C : 2 * C] = u[:, 0:W].astype(BF16)
            taps[at, :, 2 * C : 3 * C] = pltpu.roll(u, WT - 1, 1)[:, 0:W].astype(BF16)

    def conv(k):
        rows = [taps[a : a + H].reshape(PIXELS, 3 * C) for a in range(3)]
        y = jnp.dot(jnp.concatenate(rows, axis=-1), weights[k].reshape(9 * C, C), preferred_element_type=F32)
        return y.reshape(H, W, C)

    def conv_back(piece, k):
        y = None
        for a in range(3):
            for b in range(3):
                d = lax.dot_general(
                    piece(a, b), weights[k, 8 - 3 * a - b], (((1,), (1,)), ((), ())), preferred_element_type=F32
                )
                y = d if y is None else y + d
        return y.reshape(H, W, C)

    def tap(a, b):
        return taps[a : a + H, :, b * C : (b + 1) * C].reshape(PIXELS, C)

    fields[0, 1 : H + 1, 0:W, :] = latent[...].astype(F32)
    put_moments(0, latent[...].astype(F32))
    cot_copy.wait()

    def mask_row(i, carry):
        row = jnp.broadcast_to(mask[pl.ds(i, 1), :].astype(F32), (FW, FW)).T
        fine[0, i + 1, 0:FW, :] = cot[i, :, 0:128].astype(F32) * row
        fine[1, i + 1, 0:FW, :] = cot[i, :, 128:256].astype(F32) * row
        return carry

    pl.semaphore_wait(barrier, len(greeted))
    start_a(0)
    for copy in field_copies(0):
        copy.start()
    lax.fori_loop(0, FH, mask_row, 0)
    for copy in fine_copies():
        copy.start()

    def slope(k):
        mean, inv = load_stats(k)
        n = (fields[k, 1 : H + 1, 0:W, :] - mean) * inv
        s = sigmoid(n)
        slopes[k] = s * (1.0 + n * (1.0 - s))

    def boxes():
        for copy in fine_copies():
            copy.wait_recv()
        fine[:, 0] = fine[:, 0] * top
        fine[:, FH + 1] = fine[:, FH + 1] * bottom
        fine[:, :, FW : FW + 8, :] = fine[:, :, FW : FW + 8, :] * right
        fine[:, :, FWT - 8 : FWT, :] = fine[:, :, FWT - 8 : FWT, :] * left

        def columns(v_even, v_odd, dst, i):
            dst[i, :, 0:C] = (pltpu.roll(v_odd, 1, 0) + v_even)[0:W].astype(BF16)
            dst[i, :, C : 2 * C] = (v_even + v_odd)[0:W].astype(BF16)
            dst[i, :, 2 * C : 3 * C] = (v_odd + pltpu.roll(v_even, WT - 1, 0))[0:W].astype(BF16)

        def pair(i, dst, at):
            even, odd = (
                jnp.concatenate(
                    [fine[h, i, pl.ds(q, WT, 2), :] + fine[h, i + 1, pl.ds(q, WT, 2), :] for h in (0, 1)], axis=1
                )
                for q in (0, 1)
            )
            columns(even, odd, dst, at)

        def body(i, carry):
            pair(2 * i, box_a, i)
            pair(2 * i + 1, box_b, i)
            return carry

        lax.fori_loop(0, H, body, 0)
        pair(2 * H, box_a, H)

    def upper():
        up_copy.wait()

        def piece(a, b):
            at = slice(b * C, (b + 1) * C)
            if a == 1:
                return box_b[:, :, at].reshape(PIXELS, C)
            return box_a[a // 2 : a // 2 + H, :, at].reshape(PIXELS, C)

        total[1 : H + 1, 0:W, :] = conv_back(piece, 6)
        for copy in total_copies():
            copy.start()

    def finish_moments(k):
        mean, square = merge_moments(buf_b[k], PIXELS * SIDE)
        count = float(PIXELS * SIDE * SIDE)
        for step in (1, 2, 4):
            other, squares = lane_swap(mean, step), lane_swap(square, step)
            delta = mean - other
            mean = (mean + other) * 0.5
            square = square + squares + delta * delta * (count * 0.5)
            count *= 2.0
        inv = lax.rsqrt(square * (1.0 / count) + EPS)
        mean, inv = wide(mean), wide(inv)
        stats[k, 0:1, :] = mean.reshape(1, C)
        stats[k, 1:2, :] = inv.reshape(1, C)
        return mean, inv

    def forward(k, carry):
        @pl.when(k > 0)
        def _():
            start_a(k)
            for copy in field_copies(k):
                copy.start()
            slope(k - 1)

        phase_wait(buf_a.at[k], recv_a.at[k])
        mean, square = merge_moments(buf_a[k], PIXELS)
        buf_b[k, 0, 0:2, :] = mean
        buf_b[k, 0, 2:4, :] = square
        start_b(k)

        @pl.when(k == 1)
        def _():
            boxes()

        @pl.when(k == 2)
        def _():
            upper()

        @pl.when(k < 5)
        def _():
            weight_copy(k).wait()

        for copy in field_copies(k):
            copy.wait_recv()
        phase_wait(buf_b.at[k], recv_b.at[k])
        mean, inv = finish_moments(k)

        @pl.when(k < 5)
        def _():
            def active(first, rows):
                n = (fields[k, first : first + rows] - mean) * inv
                return n * sigmoid(n)

            put_taps(active)
            y = conv(k)
            keep = jnp.where(k % 2 == 1, 1.0, 0.0).astype(F32)
            y = y + keep * fields[jnp.maximum(k - 1, 0), 1 : H + 1, 0:W, :]
            fields[k + 1, 1 : H + 1, 0:W, :] = y
            put_moments(k + 1, y)

        return carry

    lax.fori_loop(0, 6, forward, 0)

    slope(5)
    weight_copy(5).wait()
    for copy in total_copies():
        copy.wait()
    put_taps(lambda first, rows: total[first : first + rows])

    def next_grad(k):
        d = conv_back(tap, k) * slopes[k]
        grads[k, 1 : H + 1, 0:W, :] = d
        mean, inv = load_stats(k)
        put_sums(11 - k, d, (fields[k, 1 : H + 1, 0:W, :] - mean) * inv)

    next_grad(5)

    def backward(j, carry):
        k = 5 - j
        t = 6 + j
        start_a(t)
        for copy in grad_copies(k):
            copy.start()
        phase_wait(buf_a.at[t], recv_a.at[t])
        buf_b[t, 0] = jnp.sum(buf_a[t], axis=0) * (1.0 / SIDE)
        start_b(t)
        for copy in grad_copies(k):
            copy.wait_recv()
        phase_wait(buf_b.at[t], recv_b.at[t])
        sums = jnp.sum(buf_b[t], axis=0) * (1.0 / (SIDE * GROUP))
        for step in (1, 2, 4):
            sums = sums + lane_swap(sums, step)
        first_mean, second_mean = wide(sums[0:2]), wide(sums[2:4])
        mean, inv = load_stats(k)
        whole = jnp.where(k % 2 == 0, 1.0, 0.0).astype(F32)

        def back(first, rows):
            at = slice(first, first + rows)
            n = (fields[k, at] - mean) * inv
            u = inv * (grads[k, at] - first_mean - n * second_mean)
            u = u + whole * total[at]

            @pl.when(k % 2 == 0)
            def _():
                total[at] = u

            return u

        put_taps(back)

        @pl.when(k > 0)
        def _():
            next_grad(k - 1)

        return carry

    lax.fori_loop(0, 6, backward, 0)
    out[...] = total[1 : H + 1, 0:W, :]

    def drain(t, carry):
        phase_wait(buf_a.at[t], send_a.at[t])
        phase_wait(buf_b.at[t], send_b.at[t])
        return carry

    lax.fori_loop(0, 12, drain, 0)

    def drain_halos(k, carry):
        for copy in field_copies(k) + grad_copies(k):
            copy.wait_send()
        return carry

    lax.fori_loop(0, 6, drain_halos, 0)
    for copy in fine_copies():
        copy.wait_send()


def per_device(latent, cotangent, pixel_mask, res_kernels, up_kernel):
    vmem = pl.BlockSpec(memory_space=pltpu.VMEM)
    hbm = pl.BlockSpec(memory_space=pl.ANY)
    dma = pltpu.SemaphoreType.DMA
    return pl.pallas_call(
        kernel,
        out_shape=jax.ShapeDtypeStruct((H, W, C), F32),
        in_specs=[vmem, vmem, hbm, hbm, hbm],
        out_specs=vmem,
        scratch_shapes=[
            pltpu.VMEM((FH, FW, C), BF16),
            pltpu.VMEM((7, 9, C, C), BF16),
            pltpu.VMEM((6, H + 2, WT, C), F32),
            pltpu.VMEM((6, H + 2, WT, C), F32),
            pltpu.VMEM((H + 2, WT, C), F32),
            pltpu.VMEM((2, FH + 2, FWT, 128), F32),
            pltpu.VMEM((6, H, W, C), F32),
            pltpu.VMEM((6, 8, C), F32),
            pltpu.VMEM((H + 2, W, 3 * C), BF16),
            pltpu.VMEM((H + 1, W, 3 * C), BF16),
            pltpu.VMEM((H, W, 3 * C), BF16),
            pltpu.VMEM((12, SIDE, 4, 128), F32),
            pltpu.VMEM((12, SIDE, 4, 128), F32),
            dma((8,)),
            dma((12,)),
            dma((12,)),
            dma((12,)),
            dma((12,)),
            dma((14, 8)),
            dma((14, 8)),
        ],
        compiler_params=pltpu.CompilerParams(
            collective_id=0, has_side_effects=True, vmem_limit_bytes=56 * 2**20
        ),
    )(
        latent,
        pixel_mask,
        cotangent,
        res_kernels.reshape(6, 9, C, C),
        up_kernel.reshape(9, C, C),
    )


def solution(mesh):
    in_specs = (P("rows", "cols", None), P("rows", "cols", None), P("rows", "cols"), P(), P())
    out_specs = P("rows", "cols", None)
    return jax.shard_map(
        per_device, mesh=mesh, in_specs=in_specs, out_specs=out_specs, check_vma=False
    )
```

time: 1650 us -> 143 us (0.09)
  blocking collectives: 1380 us -> 0 us
  Pallas kernels: 0 us -> 141 us
  starting transfers between devices: 117 us -> 0 us
  waiting for transfers between devices: 51.9 us -> 0 us
  local copies, waits for them, and re-layouts: 33.6 us -> 1.87 us
  matrix products: 31 us -> 0 us
  other arithmetic: 26.4 us -> 0 us
    psum x18 -> x0, blocking collectives: 1380 us -> none  [the longest x6 470 us: norm_forward(): average = lax.psum(jnp.sum(grouped, axis=(0, 2)), ('cols', 'rows')) / number]
    pallas_call x0 -> x1, Pallas kernels: none -> 141 us  [per_device(): pl.pallas_call(kernel, out_shape=jax.ShapeDtypeStruct((H, W, C), F32), in...]
    ppermute x48 -> x0, starting transfers between devices: 117 us -> none  [the longest x24 76.3 us: padded_2(): lax.ppermute(lax.slice_in_dim(block, block.shape[dim] - width, None, axis...]
    ppermute x48 -> x0, waiting for transfers between devices: 51.9 us -> none  [the longest x24 51.7 us: padded_2(): lax.ppermute(lax.slice_in_dim(block, 0, width, axis=dim), axis, backward)]
    conv_general_dilated x12 -> x0, matrix products: 31 us -> none  [tile_conv(): lax.conv_general_dilated(padded[None], kernel, (1, 1), 'VALID', dimension...]
  transfers between devices with their start and end apart: 48 -> 0, of which waited for: 16 -> 0; matrix products, arithmetic and copies ran while one was open for 1% -> 0% of each run, Pallas kernels for 0% -> 0%
where the time goes in v1:
time: 143 us
  Pallas kernels  141 us (99%)
  local copies, waits for them, and re-layouts  1.87 us (1%)
    pallas_call x1, Pallas kernels, per_device(): pl.pallas_call(kernel, out_shape=jax.ShapeDtypeStruct((H, W, C), F32), in...  141 us

profile of v1, /device:TPU:1, one launch (start us, length us, event | category | flops | bytes accessed | tf_op | source)
XLA Modules:
  0.0 142.9 jit_solution(7031364596158750701)
XLA Ops:
  0.0 141.1 %shard_map.55 = f32[8,64,256]{2,1,0:T(8,128)} custom-call(bf16[8,64,256]{2,1,0:T(8,128)(2,1)} %latent.1, s32[16,128]{1,0:T(8,128)} %mask.1, bf16[16,128,256]{2,1,0:T(8,128)(2,1)} %cot_hbm.1, bf16[6,9,256,256]{3,2,1,0:T(8,128)(2,1)} %bitcast.2, bf16[9,256,256]{2,1,0:T(8,128)(2,1)} %bitcast.3), custom_call_target="tpu_custom_call" | custom-call | tf_op jit(solution)/shard_map/pallas_call | solution.py:428
  141.1 1.9 %copy.7 = f32[8,64,256]{2,1,0:T(8,128)} copy(f32[8,64,256]{2,1,0:T(8,128)} %shard_map.55) | data formatting | bytes 1048576

commit v2 on v1

v2 whole, which is shorter than its diff:
```python
import functools

import jax
import jax.numpy as jnp
from jax import lax
from jax.experimental import pallas as pl
from jax.experimental.pallas import tpu as pltpu
from jax.sharding import PartitionSpec as P

LAYERS = 3
EPS = 1e-06
MESH = pl.DeviceIdType.MESH
F32 = jnp.float32
BF16 = jnp.bfloat16

H, W, C = 8, 64, 256
T = 3
RT = H + 2 * T
WT = W + 8
WB = W + 16
FH, FW = 2 * H, 2 * W
FWT = FW + 16
SIDE = 16
PIXELS = H * W
GROUP = 8


def position():
    c = lax.axis_index("cols")
    r = lax.axis_index("rows")
    core = c % 2
    chip = c // 2
    return c, r, core, chip % 4, chip // 4


def plane_peers():
    c, r, core, x, y = position()
    out = []
    for dy in range(4):
        for dx in range(4):
            if dx or dy:
                far = min(dx, 4 - dx) + min(dy, 4 - dy)
                out.append((far, dy * 4 + dx, (((y + dy) % 4) * 4 + (x + dx) % 4) * 2 + core, r))
    return [p[1:] for p in sorted(out, key=lambda p: -p[0])]


def column_peers():
    c, r, core, x, y = position()
    out = []
    for dz in range(8):
        for dc in range(2):
            if dz or dc:
                far = min(dz, 8 - dz)
                out.append((far, dz * 2 + dc, c - core + (core + dc) % 2, (r + dz) % 8))
    return [p[1:] for p in sorted(out, key=lambda p: -p[0])]


def neighbours():
    c, r, core, x, y = position()
    out = []
    for dr in (-1, 0, 1):
        for dc in (-1, 0, 1):
            if dr or dc:
                out.append((dr, dc, (c + dc + 32) % 32, (r + dr + 8) % 8))
    return out


def halo_copies(field, top, height, width, total, edges, corners, send, recv):
    def spans(step, first, size, end, near, far):
        n = far - near + 1
        if step < 0:
            return pl.ds(first + near - 1, n), pl.ds(first + size + near - 1, n)
        if step > 0:
            return pl.ds(first + size - far, n), pl.ds(end - far, n)
        return pl.ds(first, size), pl.ds(first, size)

    copies = []
    for dr, dc, col, row in neighbours():
        band = corners if dr and dc else edges
        if band is None:
            continue
        src_r, dst_r = spans(dr, top, height, top, *band)
        src_c, dst_c = spans(dc, 0, width, total, *band)
        src, dst = (src_r, src_c, slice(None)), (dst_r, dst_c, slice(None))
        if len(field.shape) == 4:
            src, dst = (slice(None),) + src, (slice(None),) + dst
        copies.append(
            pltpu.make_async_remote_copy(
                src_ref=field.at[src],
                dst_ref=field.at[dst],
                send_sem=send.at[len(copies)],
                recv_sem=recv.at[len(copies)],
                device_id={"cols": col, "rows": row},
                device_id_type=MESH,
            )
        )
    return copies


def phase_start(buf, peers, send, recv):
    for slot, col, row in peers:
        pltpu.make_async_remote_copy(
            src_ref=buf.at[0],
            dst_ref=buf.at[slot],
            send_sem=send,
            recv_sem=recv,
            device_id={"cols": col, "rows": row},
            device_id_type=MESH,
        ).start()


def phase_wait(buf, sem):
    pltpu.make_async_copy(buf.at[pl.ds(1, SIDE - 1)], buf.at[pl.ds(1, SIDE - 1)], sem).wait()


def merge_moments(parts, count):
    mean = jnp.sum(parts[:, 0:2], axis=0) * (1.0 / SIDE)
    delta = parts[:, 0:2] - mean[None]
    square = jnp.sum(parts[:, 2:4] + delta * delta * float(count), axis=0)
    return mean, square


def lane_swap(value, step):
    lane = lax.broadcasted_iota(jnp.int32, value.shape, 1)
    return jnp.where((lane & step) != 0, pltpu.roll(value, step, 1), pltpu.roll(value, 128 - step, 1))


def wide(value):
    return jnp.concatenate([value[0:1], value[1:2]], axis=1).reshape(1, 1, C)


def sigmoid(v):
    return 1.0 / (1.0 + jnp.exp(-v))


def kernel(
    latent, mask, cot_hbm, res_hbm, up_hbm, out,
    cot, weights, fields, grads, total, pre, fine, slopes, stats, taps, ones, box_a, box_b,
    buf_a, buf_b, sum_a, sum_b, cor_own, cor_a, cor_b, cor_c, cor, expanded,
    load_sem, send_a, send_b, recv_a, recv_b, csend, crecv, hsend, hrecv,
):
    c, r, _, px, py = position()
    place = py * 4 + px
    top = jnp.where(r == 0, 0.0, 1.0).astype(F32)
    bottom = jnp.where(r == 7, 0.0, 1.0).astype(F32)
    left = jnp.where(c == 0, 0.0, 1.0).astype(F32)
    right = jnp.where(c == 31, 0.0, 1.0).astype(F32)
    side = lax.broadcasted_iota(jnp.int32, (1, 8, C), 1)
    edge = jnp.where(side < 4, right, left)

    barrier = pltpu.get_barrier_semaphore()
    plane, column = plane_peers(), column_peers()
    greeted = [p[1:] for p in plane] + [p[1:] for p in column] + [p[2:] for p in neighbours()]
    for col, row in greeted:
        pl.semaphore_signal(barrier, inc=1, device_id={"cols": col, "rows": row}, device_id_type=MESH)

    def weight_copy(k):
        return pltpu.make_async_copy(res_hbm.at[k], weights.at[k], load_sem.at[k])

    up_copy = pltpu.make_async_copy(up_hbm, weights.at[6], load_sem.at[6])
    cot_copy = pltpu.make_async_copy(cot_hbm, cot, load_sem.at[7])
    cot_copy.start()
    weight_copy(0).start()
    up_copy.start()
    for k in range(1, 6):
        weight_copy(k).start()

    def load_stats(k):
        return stats[k, 0:1, :].reshape(1, 1, C), stats[k, 1:2, :].reshape(1, 1, C)

    def normed(k, rows, columns=slice(0, WT)):
        mean, inv = load_stats(k)
        return (fields[k, rows, columns, :] - mean) * inv

    tile_rows, tile_columns = slice(T, T + H), slice(0, W)

    def put_rows(buf, at, first, second):
        buf[at : at + 1, :] = first[:, 0:128]
        buf[at + 1 : at + 2, :] = first[:, 128:256]
        buf[at + 2 : at + 3, :] = second[:, 0:128]
        buf[at + 3 : at + 4, :] = second[:, 128:256]

    def put_moments(k, x):
        mean = jnp.sum(x, axis=(0, 1)).reshape(1, C) * (1.0 / PIXELS)
        delta = x - mean.reshape(1, 1, C)
        square = jnp.sum(delta * delta, axis=(0, 1)).reshape(1, C)
        put_rows(buf_a.at[k, 0], 0, mean, square)

    def put_sums(l, at, d, n):
        first = jnp.sum(d, axis=(0, 1)).reshape(1, C) * (1.0 / PIXELS)
        second = jnp.sum(d * n, axis=(0, 1)).reshape(1, C) * (1.0 / PIXELS)
        put_rows(sum_a.at[l, 0], at, first, second)

    def ring_copies(k):
        return halo_copies(fields.at[k], T, H, W, WT, (1, 1), (1, 3), hsend.at[k], hrecv.at[k])

    def wide_copies(k):
        return halo_copies(fields.at[k], T, H, W, WT, (2, 3), None, hsend.at[k + 6], hrecv.at[k + 6])

    def grad_copies(l):
        return halo_copies(grads.at[l], T, H, W, WT, (1, 3), (1, 3), hsend.at[l + 12], hrecv.at[l + 12])

    def total_copies():
        return halo_copies(total, T, H, W, WT, (1, 2), (1, 2), hsend.at[15], hrecv.at[15])

    def fine_copies():
        return halo_copies(fine, 1, FH, FW, FWT, (1, 1), (1, 1), hsend.at[16], hrecv.at[16])

    def put_taps(make, first, last, columns):
        parts = ((first, T, top), (T, T + H, None), (T + H, last, bottom))
        for begin, end, scale in parts:
            u = make(begin, end - begin)
            if scale is not None:
                u = u * scale
            u = jnp.concatenate([u[:, 0:W], u[:, W:WT] * edge], axis=1)
            at = slice(begin - first, end - first)
            for b, v in enumerate((pltpu.roll(u, 1, 1), u, pltpu.roll(u, WT - 1, 1))):
                if columns > WT:
                    v = jnp.concatenate([v, jnp.zeros((end - begin, columns - WT, C), F32)], axis=1)
                taps[at, 0:columns, b * C : (b + 1) * C] = v[:, 0:columns].astype(BF16)

    def conv(k):
        rows = [taps[a : a + H, 0:W].reshape(PIXELS, 3 * C) for a in range(3)]
        y = jnp.dot(jnp.concatenate(rows, axis=-1), weights[k].reshape(9 * C, C), preferred_element_type=F32)
        return y.reshape(H, W, C)

    def conv_back(piece, k, rows, columns):
        y = None
        for a in range(3):
            for b in range(3):
                d = lax.dot_general(
                    piece(a, b), weights[k, 8 - 3 * a - b], (((1,), (1,)), ((), ())), preferred_element_type=F32
                )
                y = d if y is None else y + d
        return y.reshape(rows, columns, C)

    def tap_conv_back(k, rows, columns):
        def piece(a, b):
            return taps[a : a + rows, 0:columns, b * C : (b + 1) * C].reshape(rows * columns, C)

        return conv_back(piece, k, rows, columns)

    fields[0, tile_rows, tile_columns, :] = latent[...].astype(F32)
    put_moments(0, latent[...].astype(F32))

    def start_a(k):
        phase_start(buf_a.at[k], plane, send_a.at[k], recv_a.at[k])
        for copy in ring_copies(k) + wide_copies(k):
            copy.start()

    pl.semaphore_wait(barrier, len(greeted))
    start_a(0)
    cot_copy.wait()

    def mask_row(i, carry):
        row = jnp.broadcast_to(mask[pl.ds(i, 1), :].astype(F32), (FW, FW)).T
        fine[0, i + 1, 0:FW, :] = cot[i, :, 0:128].astype(F32) * row
        fine[1, i + 1, 0:FW, :] = cot[i, :, 128:256].astype(F32) * row
        return carry

    lax.fori_loop(0, FH, mask_row, 0)
    for copy in fine_copies():
        copy.start()

    inside = jnp.concatenate(
        [
            jnp.full((1, W + 16, 128), 1.0, F32) * top,
            jnp.full((H, W + 16, 128), 1.0, F32),
            jnp.full((1, W + 16, 128), 1.0, F32) * bottom,
        ],
        axis=0,
    )
    column_at = lax.broadcasted_iota(jnp.int32, (H + 2, W, 128), 1)
    for b, scale in enumerate((jnp.where(column_at == 0, left, 1.0), None, jnp.where(column_at == W - 1, right, 1.0))):
        v = inside[:, 0:W] if scale is None else inside[:, 0:W] * scale
        ones[:, :, b * 128 : (b + 1) * 128] = v.astype(BF16)

    def slope(k, first, last):
        n = normed(k, slice(first, last))
        s = sigmoid(n)
        slopes[k, first - 1 : last - 1] = s * (1.0 + n * (1.0 - s))

    def boxes():
        for copy in fine_copies():
            copy.wait_recv()
        fine[:, 0] = fine[:, 0] * top
        fine[:, FH + 1] = fine[:, FH + 1] * bottom
        fine[:, :, FW : FW + 8, :] = fine[:, :, FW : FW + 8, :] * right
        fine[:, :, FWT - 8 : FWT, :] = fine[:, :, FWT - 8 : FWT, :] * left

        def pair(i, dst, at):
            even, odd = (
                jnp.concatenate(
                    [fine[h, i, pl.ds(q, WT, 2), :] + fine[h, i + 1, pl.ds(q, WT, 2), :] for h in (0, 1)], axis=1
                )
                for q in (0, 1)
            )
            dst[at, :, 0:C] = (pltpu.roll(odd, 1, 0) + even)[0:W].astype(BF16)
            dst[at, :, C : 2 * C] = (even + odd)[0:W].astype(BF16)
            dst[at, :, 2 * C : 3 * C] = (odd + pltpu.roll(even, WT - 1, 0))[0:W].astype(BF16)

        def body(i, carry):
            pair(2 * i, box_a, i)
            pair(2 * i + 1, box_b, i)
            return carry

        lax.fori_loop(0, H, body, 0)
        pair(2 * H, box_a, H)

    def upper():
        up_copy.wait()

        def piece(a, b):
            at = slice(b * C, (b + 1) * C)
            if a == 1:
                return box_b[:, :, at].reshape(PIXELS, C)
            return box_a[a // 2 : a // 2 + H, :, at].reshape(PIXELS, C)

        total[tile_rows, tile_columns, :] = conv_back(piece, 6, H, W)
        for copy in total_copies():
            copy.start()

    def lift(k):
        put_taps(lambda first, rows: total[first : first + rows], T - 2, T + H + 2, WB)
        pre[...] = tap_conv_back(k, H + 2, WB)[:, 0:WT]

    def correlate(l):
        k = 2 * l
        mean = jnp.concatenate([buf_a[k + 1, 0, 0:1, :], buf_a[k + 1, 0, 1:2, :]], axis=1)
        put_taps(
            lambda first, rows: fields[k + 1, first : first + rows] - mean.reshape(1, 1, C), T - 1, T + H + 1, W
        )
        cor[...] = jnp.zeros_like(cor)

        def kind(i, carry):
            n = normed(k, tile_rows, tile_columns)
            q = slopes[k, T - 1 : T - 1 + H, 0:W] * jnp.where(i == 0, 1.0, n)
            q = q.reshape(PIXELS, C).astype(BF16)
            raw = plain = None
            for a in range(3):
                for b in range(3):
                    weight = weights[k, 8 - 3 * a - b].astype(F32)
                    over = (((0,), (0,)), ((), ()))
                    field = taps[a : a + H, 0:W, b * C : (b + 1) * C].reshape(PIXELS, C)
                    first = lax.dot_general(q, field, over, preferred_element_type=F32) * weight
                    unit = ones[a : a + H, :, b * 128 : (b + 1) * 128].reshape(PIXELS, 128)
                    second = lax.dot_general(q, unit, over, preferred_element_type=F32)
                    second = jnp.concatenate([second, second], axis=1) * weight
                    raw = first if raw is None else raw + first
                    plain = second if plain is None else plain + second
            raw = raw + plain * mean
            row = lax.broadcasted_iota(jnp.int32, (C, 128), 0) // GROUP
            lane = lax.broadcasted_iota(jnp.int32, (C, 128), 1)
            for j, block in enumerate((raw, plain)):
                block = jnp.sum(block.reshape(C // GROUP, GROUP, C), axis=1) * (1.0 / (PIXELS * SIDE * SIDE * GROUP))
                pick = jnp.where(lane == 64 * i + 32 * j + row, 1.0, 0.0).astype(F32)
                cor[...] += jnp.dot(block, pick, precision=lax.Precision.HIGHEST, preferred_element_type=F32)
            return carry

        lax.fori_loop(0, 2, kind, 0)
        for i in range(SIDE):
            cor_own[l, i] = cor[2 * i : 2 * i + 2, :]
        for slot, col, row in plane:
            x, y = (col // 2) % 4, col // 8
            pltpu.make_async_remote_copy(
                src_ref=cor_own.at[l, y * 4 + x],
                dst_ref=cor_a.at[l, slot],
                send_sem=csend.at[l],
                recv_sem=crecv.at[l],
                device_id={"cols": col, "rows": row},
                device_id_type=MESH,
            ).start()

    def correlate_b(l):
        phase_wait(cor_a.at[l], crecv.at[l])
        cor_b[l, 0] = cor_own[l, place] + jnp.sum(cor_a[l, 1:SIDE], axis=0)
        phase_start(cor_b.at[l], column, csend.at[l + 3], crecv.at[l + 3])

    def correlate_c(l):
        phase_wait(cor_b.at[l], crecv.at[l + 3])
        cor_c[l, place] = jnp.sum(cor_b[l], axis=0)
        for slot, col, row in plane:
            pltpu.make_async_remote_copy(
                src_ref=cor_c.at[l, place],
                dst_ref=cor_c.at[l, place],
                send_sem=csend.at[l + 6],
                recv_sem=crecv.at[l + 6],
                device_id={"cols": col, "rows": row},
                device_id_type=MESH,
            ).start()

    def expand(l):
        phase_wait(cor_c.at[l], crecv.at[l + 6])
        for i in range(SIDE):
            cor[2 * i : 2 * i + 2, :] = cor_c[l, i]
        whole = cor[...]
        high = whole.astype(BF16)
        low = (whole - high.astype(F32)).astype(BF16)
        group = lax.broadcasted_iota(jnp.int32, (32, C), 1) // GROUP
        spread = jnp.where(lax.broadcasted_iota(jnp.int32, (32, C), 0) == group, 1.0, 0.0).astype(BF16)
        lane = lax.broadcasted_iota(jnp.int32, (128, C), 0)
        channel = lax.broadcasted_iota(jnp.int32, (128, C), 1) // GROUP
        for i in range(2):
            for j in range(2):
                pick = jnp.where(lane == 64 * i + 32 * j + channel, 1.0, 0.0).astype(BF16)
                for part, value in enumerate((high, low)):
                    block = jnp.dot(value, pick, preferred_element_type=F32).astype(BF16)
                    block = lax.dot_general(
                        block, spread, (((0,), (0,)), ((), ())), preferred_element_type=F32
                    )
                    expanded[part, j * C : (j + 1) * C, i * C : (i + 1) * C] = block.astype(BF16)

    def finish_moments(k):
        mean, square = merge_moments(buf_b[k], PIXELS * SIDE)
        count = float(PIXELS * SIDE * SIDE)
        for step in (1, 2, 4):
            other, squares = lane_swap(mean, step), lane_swap(square, step)
            delta = mean - other
            mean = (mean + other) * 0.5
            square = square + squares + delta * delta * (count * 0.5)
            count *= 2.0
        inv = lax.rsqrt(square * (1.0 / count) + EPS)
        mean, inv = wide(mean), wide(inv)
        stats[k, 0:1, :] = mean.reshape(1, C)
        stats[k, 1:2, :] = inv.reshape(1, C)
        return mean, inv

    def forward(k, carry):
        @pl.when(k > 0)
        def _():
            start_a(k)
            slope(k - 1, 1, RT - 1)

        @pl.when((k == 2) | (k == 4))
        def _():
            correlate_b(k // 2 - 1)

        phase_wait(buf_a.at[k], recv_a.at[k])
        mean, square = merge_moments(buf_a[k], PIXELS)
        buf_b[k, 0, 0:2, :] = mean
        buf_b[k, 0, 2:4, :] = square
        phase_start(buf_b.at[k], column, send_b.at[k], recv_b.at[k])

        for copy in ring_copies(k) + wide_copies(k)[1:3]:
            copy.wait_recv()

        @pl.when(k % 2 == 1)
        def _():
            correlate(k // 2)

        @pl.when((k == 2) | (k == 4))
        def _():
            correlate_c(k // 2 - 1)

        @pl.when(k == 2)
        def _():
            boxes()
            upper()

        @pl.when(k == 4)
        def _():
            weight_copy(5).wait()
            for copy in total_copies():
                copy.wait()
            lift(5)

        @pl.when(k < 5)
        def _():
            weight_copy(k).wait()

        for copy in wide_copies(k)[0::3]:
            copy.wait_recv()
        phase_wait(buf_b.at[k], recv_b.at[k])
        mean, inv = finish_moments(k)

        @pl.when(k < 5)
        def _():
            def active(first, rows):
                n = (fields[k, first : first + rows] - mean) * inv
                return n * sigmoid(n)

            put_taps(active, T - 1, T + H + 1, W)
            y = conv(k)
            keep = jnp.where(k % 2 == 1, 1.0, 0.0).astype(F32)
            y = y + keep * fields[jnp.maximum(k - 1, 0), tile_rows, tile_columns, :]
            fields[k + 1, tile_rows, tile_columns, :] = y
            put_moments(k + 1, y)

        return carry

    lax.fori_loop(0, 6, forward, 0)
    slope(5, T - 1, T + H + 1)

    def layer(l, last):
        k = 2 * l
        mean1, inv1 = load_stats(k)
        mean2, inv2 = load_stats(k + 1)
        t = 8 - l
        grads[l, tile_rows, tile_columns, :] = (
            pre[1 : H + 1, 0:W] * slopes[k + 1, T - 1 : T - 1 + H, 0:W]
        )
        put_sums(l, 0, grads[l, tile_rows, tile_columns, :], normed(k + 1, tile_rows, tile_columns))

        def unprojected(first, rows):
            at = first - T + 1
            return inv2 * (pre[at : at + rows] * slopes[k + 1, first - 1 : first - 1 + rows])

        put_taps(unprojected, T - 1, T + H + 1, W)
        d = tap_conv_back(k, H, W) * slopes[k, T - 1 : T - 1 + H, 0:W]
        put_sums(l, 4, d, normed(k, tile_rows, tile_columns))
        phase_start(sum_a.at[l], plane, send_a.at[t], recv_a.at[t])
        for copy in grad_copies(l):
            copy.start()

        @pl.when(l == 2)
        def _():
            correlate_b(l)

        phase_wait(sum_a.at[l], recv_a.at[t])
        sum_b[l, 0] = jnp.sum(sum_a[l], axis=0) * (1.0 / SIDE)
        phase_start(sum_b.at[l], column, send_b.at[t], recv_b.at[t])

        @pl.when(l == 2)
        def _():
            correlate_c(l)

        expand(l)
        for copy in grad_copies(l):
            copy.wait_recv()
        phase_wait(sum_b.at[l], recv_b.at[t])
        sums = jnp.sum(sum_b[l], axis=0) * (1.0 / (SIDE * GROUP))
        for step in (1, 2, 4):
            sums = sums + lane_swap(sums, step)
        first2, second2, first1, second1 = (wide(sums[i : i + 2]) for i in (0, 2, 4, 6))
        scaled = inv2 * second2
        source = jnp.concatenate([inv2 * scaled, inv2 * (first2 - mean2 * scaled)], axis=-1).reshape(1, 2 * C)
        source = jnp.broadcast_to(source * (1.0 / GROUP), (16, 2 * C))
        high = source.astype(BF16)
        low = (source - high.astype(F32)).astype(BF16)
        moved = (
            jnp.dot(high, expanded[0], preferred_element_type=F32)
            + jnp.dot(low, expanded[0], preferred_element_type=F32)
            + jnp.dot(high, expanded[1], preferred_element_type=F32)
        )
        first1 = first1 - moved[0:1, 0:C].reshape(1, 1, C)
        second1 = second1 - moved[0:1, C : 2 * C].reshape(1, 1, C)

        def back(first, rows):
            at = slice(first, first + rows)
            return inv2 * (grads[l, at] - first2 - normed(k + 1, at) * second2)

        if last:
            put_taps(back, T - 1, T + H + 1, W)
            d = tap_conv_back(k, H, W) * slopes[k, T - 1 : T - 1 + H, 0:W]
            n = normed(k, tile_rows, tile_columns)
            out[...] = total[tile_rows, tile_columns, :] + inv1 * (d - first1 - n * second1)
        else:
            put_taps(back, 0, RT, WB)
            d = tap_conv_back(k, H + 4, WB)[:, 0:WT] * slopes[k]
            rows = slice(T - 2, T + H + 2)
            total[rows] += inv1 * (d - first1 - normed(k, rows) * second1)
            lift(k - 1)

    def backward(j, carry):
        layer(2 - j, False)
        return carry

    lax.fori_loop(0, 2, backward, 0)
    layer(0, True)

    def drain(k, carry):
        phase_wait(buf_a.at[k], send_a.at[k])
        phase_wait(buf_b.at[k], send_b.at[k])
        for copy in ring_copies(k) + wide_copies(k):
            copy.wait_send()
        return carry

    lax.fori_loop(0, 6, drain, 0)

    def drain_back(l, carry):
        phase_wait(sum_a.at[l], send_a.at[8 - l])
        phase_wait(sum_b.at[l], send_b.at[8 - l])
        phase_wait(cor_a.at[l], csend.at[l])
        phase_wait(cor_b.at[l], csend.at[l + 3])
        phase_wait(cor_c.at[l], csend.at[l + 6])
        for copy in grad_copies(l):
            copy.wait_send()
        return carry

    lax.fori_loop(0, 3, drain_back, 0)
    for copy in fine_copies():
        copy.wait_send()


def per_device(latent, cotangent, pixel_mask, res_kernels, up_kernel):
    vmem = pl.BlockSpec(memory_space=pltpu.VMEM)
    hbm = pl.BlockSpec(memory_space=pl.ANY)
    dma = pltpu.SemaphoreType.DMA
    return pl.pallas_call(
        kernel,
        out_shape=jax.ShapeDtypeStruct((H, W, C), F32),
        in_specs=[vmem, vmem, hbm, hbm, hbm],
        out_specs=vmem,
        scratch_shapes=[
            pltpu.VMEM((FH, FW, C), BF16),
            pltpu.VMEM((7, 9, C, C), BF16),
            pltpu.VMEM((6, RT, WT, C), F32),
            pltpu.VMEM((3, RT, WT, C), F32),
            pltpu.VMEM((RT, WT, C), F32),
            pltpu.VMEM((H + 2, WT, C), F32),
            pltpu.VMEM((2, FH + 2, FWT, 128), F32),
            pltpu.VMEM((6, RT - 2, WT, C), F32),
            pltpu.VMEM((6, 8, C), F32),
            pltpu.VMEM((RT, WB, 3 * C), BF16),
            pltpu.VMEM((H + 2, W, 3 * 128), BF16),
            pltpu.VMEM((H + 1, W, 3 * C), BF16),
            pltpu.VMEM((H, W, 3 * C), BF16),
            pltpu.VMEM((6, SIDE, 4, 128), F32),
            pltpu.VMEM((6, SIDE, 4, 128), F32),
            pltpu.VMEM((3, SIDE, 8, 128), F32),
            pltpu.VMEM((3, SIDE, 8, 128), F32),
            pltpu.VMEM((3, SIDE, 2, 128), F32),
            pltpu.VMEM((3, SIDE, 2, 128), F32),
            pltpu.VMEM((3, SIDE, 2, 128), F32),
            pltpu.VMEM((3, SIDE, 2, 128), F32),
            pltpu.VMEM((32, 128), F32),
            pltpu.VMEM((2, 2 * C, 2 * C), BF16),
            dma((8,)),
            dma((9,)),
            dma((9,)),
            dma((9,)),
            dma((9,)),
            dma((9,)),
            dma((9,)),
            dma((17, 8)),
            dma((17, 8)),
        ],
        compiler_params=pltpu.CompilerParams(
            collective_id=0, has_side_effects=True, vmem_limit_bytes=56 * 2**20
        ),
    )(
        latent,
        pixel_mask,
        cotangent,
        res_kernels.reshape(6, 9, C, C),
        up_kernel.reshape(9, C, C),
    )


def solution(mesh):
    in_specs = (P("rows", "cols", None), P("rows", "cols", None), P("rows", "cols"), P(), P())
    out_specs = P("rows", "cols", None)
    return jax.shard_map(
        per_device, mesh=mesh, in_specs=in_specs, out_specs=out_specs, check_vma=False
    )
```

time: 143 us -> 137 us (0.958)
  Pallas kernels: 141 us -> 135 us
    pallas_call x1, Pallas kernels: 141 us -> 135 us  [per_device(): pl.pallas_call(kernel, out_shape=jax.ShapeDtypeStruct((H, W, C), F32), in...]
where the time goes in v2:
time: 137 us
  Pallas kernels  135 us (99%)
  local copies, waits for them, and re-layouts  1.87 us (1%)
    pallas_call x1, Pallas kernels, per_device(): pl.pallas_call(kernel, out_shape=jax.ShapeDtypeStruct((H, W, C), F32), in...  135 us

profile of v2, /device:TPU:1, one launch (start us, length us, event | category | flops | bytes accessed | tf_op | source)
XLA Modules:
  0.0 136.7 jit_solution(14116957128199229313)
XLA Ops:
  0.0 134.8 %shard_map.55 = f32[8,64,256]{2,1,0:T(8,128)} custom-call(bf16[8,64,256]{2,1,0:T(8,128)(2,1)} %latent.1, s32[16,128]{1,0:T(8,128)} %mask.1, bf16[16,128,256]{2,1,0:T(8,128)(2,1)} %cot_hbm.1, bf16[6,9,256,256]{3,2,1,0:T(8,128)(2,1)} %bitcast.2, bf16[9,256,256]{2,1,0:T(8,128)(2,1)} %bitcast.3), custom_call_target="tpu_custom_call" | custom-call | tf_op jit(solution)/shard_map/pallas_call | solution.py:599
  134.8 1.9 %copy.7 = f32[8,64,256]{2,1,0:T(8,128)} copy(f32[8,64,256]{2,1,0:T(8,128)} %shard_map.55) | data formatting | bytes 1048576

commit v3 on v2

--- a/solution.py
+++ b/solution.py
@@ -134,8 +134,8 @@
 
 
 def kernel(
-    latent, mask, cot_hbm, res_hbm, up_hbm, out,
-    cot, weights, fields, grads, total, pre, fine, slopes, stats, taps, ones, box_a, box_b,
+    mask, latent_hbm, cot_hbm, res_hbm, up_hbm, out,
+    latent, cot, weights, fields, grads, total, pre, fine, slopes, stats, taps, taps_n, box_a, box_b,
     buf_a, buf_b, sum_a, sum_b, cor_own, cor_a, cor_b, cor_c, cor, expanded,
     load_sem, send_a, send_b, recv_a, recv_b, csend, crecv, hsend, hrecv,
 ):
@@ -148,17 +148,19 @@
     side = lax.broadcasted_iota(jnp.int32, (1, 8, C), 1)
     edge = jnp.where(side < 4, right, left)
 
+    def weight_copy(k):
+        return pltpu.make_async_copy(res_hbm.at[k], weights.at[k], load_sem.at[k])
+
+    up_copy = pltpu.make_async_copy(up_hbm, weights.at[6], load_sem.at[6])
+    cot_copy = pltpu.make_async_copy(cot_hbm, cot, load_sem.at[7])
+    latent_copy = pltpu.make_async_copy(latent_hbm, latent, load_sem.at[8])
+    latent_copy.start()
     barrier = pltpu.get_barrier_semaphore()
     plane, column = plane_peers(), column_peers()
     greeted = [p[1:] for p in plane] + [p[1:] for p in column] + [p[2:] for p in neighbours()]
     for col, row in greeted:
         pl.semaphore_signal(barrier, inc=1, device_id={"cols": col, "rows": row}, device_id_type=MESH)
 
-    def weight_copy(k):
-        return pltpu.make_async_copy(res_hbm.at[k], weights.at[k], load_sem.at[k])
-
-    up_copy = pltpu.make_async_copy(up_hbm, weights.at[6], load_sem.at[6])
-    cot_copy = pltpu.make_async_copy(cot_hbm, cot, load_sem.at[7])
     cot_copy.start()
     weight_copy(0).start()
     up_copy.start()
@@ -206,7 +208,7 @@
     def fine_copies():
         return halo_copies(fine, 1, FH, FW, FWT, (1, 1), (1, 1), hsend.at[16], hrecv.at[16])
 
-    def put_taps(make, first, last, columns):
+    def put_taps(make, first, last, columns, dst=taps):
         parts = ((first, T, top), (T, T + H, None), (T + H, last, bottom))
         for begin, end, scale in parts:
             u = make(begin, end - begin)
@@ -217,7 +219,7 @@
             for b, v in enumerate((pltpu.roll(u, 1, 1), u, pltpu.roll(u, WT - 1, 1))):
                 if columns > WT:
                     v = jnp.concatenate([v, jnp.zeros((end - begin, columns - WT, C), F32)], axis=1)
-                taps[at, 0:columns, b * C : (b + 1) * C] = v[:, 0:columns].astype(BF16)
+                dst[at, 0:columns, b * C : (b + 1) * C] = v[:, 0:columns].astype(BF16)
 
     def conv(k):
         rows = [taps[a : a + H, 0:W].reshape(PIXELS, 3 * C) for a in range(3)]
@@ -235,16 +237,24 @@
         return y.reshape(rows, columns, C)
 
     def tap_conv_back(k, rows, columns):
-        def piece(a, b):
-            return taps[a : a + rows, 0:columns, b * C : (b + 1) * C].reshape(rows * columns, C)
-
-        return conv_back(piece, k, rows, columns)
-
+        parts = []
+        chunks = 1 if rows * columns <= PIXELS else 2
+        height = rows // chunks
+        for begin in range(0, rows, height):
+
+            def piece(a, b):
+                at = slice(begin + a, begin + a + height)
+                return taps[at, 0:columns, b * C : (b + 1) * C].reshape(height * columns, C)
+
+            parts.append(conv_back(piece, k, height, columns))
+        return parts[0] if chunks == 1 else jnp.concatenate(parts, axis=0)
+
+    latent_copy.wait()
     fields[0, tile_rows, tile_columns, :] = latent[...].astype(F32)
     put_moments(0, latent[...].astype(F32))
 
     def start_a(k):
-        phase_start(buf_a.at[k], plane, send_a.at[k], recv_a.at[k])
+        phase_start(buf_a.at[k], column, send_a.at[k], recv_a.at[k])
         for copy in ring_copies(k) + wide_copies(k):
             copy.start()
 
@@ -261,19 +271,6 @@
     lax.fori_loop(0, FH, mask_row, 0)
     for copy in fine_copies():
         copy.start()
-
-    inside = jnp.concatenate(
-        [
-            jnp.full((1, W + 16, 128), 1.0, F32) * top,
-            jnp.full((H, W + 16, 128), 1.0, F32),
-            jnp.full((1, W + 16, 128), 1.0, F32) * bottom,
-        ],
-        axis=0,
-    )
-    column_at = lax.broadcasted_iota(jnp.int32, (H + 2, W, 128), 1)
-    for b, scale in enumerate((jnp.where(column_at == 0, left, 1.0), None, jnp.where(column_at == W - 1, right, 1.0))):
-        v = inside[:, 0:W] if scale is None else inside[:, 0:W] * scale
-        ones[:, :, b * 128 : (b + 1) * 128] = v.astype(BF16)
 
     def slope(k, first, last):
         n = normed(k, slice(first, last))
@@ -327,37 +324,42 @@
     def correlate(l):
         k = 2 * l
         mean = jnp.concatenate([buf_a[k + 1, 0, 0:1, :], buf_a[k + 1, 0, 1:2, :]], axis=1)
-        put_taps(
-            lambda first, rows: fields[k + 1, first : first + rows] - mean.reshape(1, 1, C), T - 1, T + H + 1, W
-        )
-        cor[...] = jnp.zeros_like(cor)
-
-        def kind(i, carry):
-            n = normed(k, tile_rows, tile_columns)
-            q = slopes[k, T - 1 : T - 1 + H, 0:W] * jnp.where(i == 0, 1.0, n)
-            q = q.reshape(PIXELS, C).astype(BF16)
-            raw = plain = None
+
+        def plain_slope(first, rows):
+            return slopes[k, first - 1 : first - 1 + rows]
+
+        def normed_slope(first, rows):
+            return slopes[k, first - 1 : first - 1 + rows] * normed(k, slice(first, first + rows))
+
+        put_taps(plain_slope, T - 1, T + H + 1, W)
+        put_taps(normed_slope, T - 1, T + H + 1, W, taps_n)
+        x = (fields[k + 1, tile_rows, tile_columns, :] - mean.reshape(1, 1, C)).reshape(PIXELS, C).astype(BF16)
+        raw = plain = None
+        for b in range(3):
+            at = slice(b * C, (b + 1) * C)
+            sums = [jnp.sum(src[0 : H + 2, 0:W, at].astype(F32), axis=1) for src in (taps, taps_n)]
             for a in range(3):
-                for b in range(3):
-                    weight = weights[k, 8 - 3 * a - b].astype(F32)
-                    over = (((0,), (0,)), ((), ()))
-                    field = taps[a : a + H, 0:W, b * C : (b + 1) * C].reshape(PIXELS, C)
-                    first = lax.dot_general(q, field, over, preferred_element_type=F32) * weight
-                    unit = ones[a : a + H, :, b * 128 : (b + 1) * 128].reshape(PIXELS, 128)
-                    second = lax.dot_general(q, unit, over, preferred_element_type=F32)
-                    second = jnp.concatenate([second, second], axis=1) * weight
-                    raw = first if raw is None else raw + first
-                    plain = second if plain is None else plain + second
-            raw = raw + plain * mean
-            row = lax.broadcasted_iota(jnp.int32, (C, 128), 0) // GROUP
-            lane = lax.broadcasted_iota(jnp.int32, (C, 128), 1)
-            for j, block in enumerate((raw, plain)):
-                block = jnp.sum(block.reshape(C // GROUP, GROUP, C), axis=1) * (1.0 / (PIXELS * SIDE * SIDE * GROUP))
-                pick = jnp.where(lane == 64 * i + 32 * j + row, 1.0, 0.0).astype(F32)
-                cor[...] += jnp.dot(block, pick, precision=lax.Precision.HIGHEST, preferred_element_type=F32)
-            return carry
-
-        lax.fori_loop(0, 2, kind, 0)
+                weight = weights[k, 3 * a + b].astype(F32).T
+                weight = jnp.concatenate([weight, weight], axis=1)
+                q = jnp.concatenate(
+                    [src[a : a + H, 0:W, at].reshape(PIXELS, C) for src in (taps, taps_n)], axis=1
+                )
+                first = lax.dot_general(x, q, (((0,), (0,)), ((), ())), preferred_element_type=F32) * weight
+                total_q = jnp.concatenate([jnp.sum(v[a : a + H], axis=0, keepdims=True) for v in sums], axis=1)
+                second = total_q * weight
+                raw = first if raw is None else raw + first
+                plain = second if plain is None else plain + second
+        shift = jnp.broadcast_to(mean, (8, C)).T[:, 0:1]
+        raw = raw + plain * shift
+        row = lax.broadcasted_iota(jnp.int32, (2 * C, 128), 0) // GROUP
+        lane = lax.broadcasted_iota(jnp.int32, (2 * C, 128), 1)
+        whole = None
+        for j, block in enumerate((raw, plain)):
+            block = jnp.sum(block.reshape(C // GROUP, GROUP, 2 * C), axis=1) * (1.0 / (PIXELS * SIDE * SIDE * GROUP))
+            pick = jnp.where(lane == 64 * j + row, 1.0, 0.0).astype(F32)
+            part = jnp.dot(block, pick, precision=lax.Precision.HIGHEST, preferred_element_type=F32)
+            whole = part if whole is None else whole + part
+        cor[...] = whole
         for i in range(SIDE):
             cor_own[l, i] = cor[2 * i : 2 * i + 2, :]
         for slot, col, row in plane:
@@ -398,17 +400,14 @@
         low = (whole - high.astype(F32)).astype(BF16)
         group = lax.broadcasted_iota(jnp.int32, (32, C), 1) // GROUP
         spread = jnp.where(lax.broadcasted_iota(jnp.int32, (32, C), 0) == group, 1.0, 0.0).astype(BF16)
-        lane = lax.broadcasted_iota(jnp.int32, (128, C), 0)
-        channel = lax.broadcasted_iota(jnp.int32, (128, C), 1) // GROUP
-        for i in range(2):
-            for j in range(2):
-                pick = jnp.where(lane == 64 * i + 32 * j + channel, 1.0, 0.0).astype(BF16)
-                for part, value in enumerate((high, low)):
-                    block = jnp.dot(value, pick, preferred_element_type=F32).astype(BF16)
-                    block = lax.dot_general(
-                        block, spread, (((0,), (0,)), ((), ())), preferred_element_type=F32
-                    )
-                    expanded[part, j * C : (j + 1) * C, i * C : (i + 1) * C] = block.astype(BF16)
+        lane = lax.broadcasted_iota(jnp.int32, (128, 2 * C), 0)
+        channel = lax.broadcasted_iota(jnp.int32, (128, 2 * C), 1) // GROUP
+        for j in range(2):
+            pick = jnp.where(lane == 64 * j + channel, 1.0, 0.0).astype(BF16)
+            for part, value in enumerate((high, low)):
+                block = jnp.dot(value, pick, preferred_element_type=F32).astype(BF16)
+                block = lax.dot_general(spread, block, (((0,), (0,)), ((), ())), preferred_element_type=F32)
+                expanded[part, j * C : (j + 1) * C, :] = block.astype(BF16)
 
     def finish_moments(k):
         mean, square = merge_moments(buf_b[k], PIXELS * SIDE)
@@ -431,26 +430,23 @@
             start_a(k)
             slope(k - 1, 1, RT - 1)
 
+        @pl.when(k % 2 == 1)
+        def _():
+            correlate(k // 2)
+
         @pl.when((k == 2) | (k == 4))
         def _():
-            correlate_b(k // 2 - 1)
+            correlate_c(k // 2 - 1)
 
         phase_wait(buf_a.at[k], recv_a.at[k])
         mean, square = merge_moments(buf_a[k], PIXELS)
         buf_b[k, 0, 0:2, :] = mean
         buf_b[k, 0, 2:4, :] = square
-        phase_start(buf_b.at[k], column, send_b.at[k], recv_b.at[k])
-
-        for copy in ring_copies(k) + wide_copies(k)[1:3]:
-            copy.wait_recv()
+        phase_start(buf_b.at[k], plane, send_b.at[k], recv_b.at[k])
 
         @pl.when(k % 2 == 1)
         def _():
-            correlate(k // 2)
-
-        @pl.when((k == 2) | (k == 4))
-        def _():
-            correlate_c(k // 2 - 1)
+            correlate_b(k // 2)
 
         @pl.when(k == 2)
         def _():
@@ -468,7 +464,7 @@
         def _():
             weight_copy(k).wait()
 
-        for copy in wide_copies(k)[0::3]:
+        for copy in ring_copies(k) + wide_copies(k):
             copy.wait_recv()
         phase_wait(buf_b.at[k], recv_b.at[k])
         mean, inv = finish_moments(k)
@@ -490,6 +486,13 @@
 
     lax.fori_loop(0, 6, forward, 0)
     slope(5, T - 1, T + H + 1)
+
+    def drain(k, carry):
+        phase_wait(buf_a.at[k], send_a.at[k])
+        phase_wait(buf_b.at[k], send_b.at[k])
+        for copy in ring_copies(k) + wide_copies(k):
+            copy.wait_send()
+        return carry
 
     def layer(l, last):
         k = 2 * l
@@ -508,23 +511,25 @@
         put_taps(unprojected, T - 1, T + H + 1, W)
         d = tap_conv_back(k, H, W) * slopes[k, T - 1 : T - 1 + H, 0:W]
         put_sums(l, 4, d, normed(k, tile_rows, tile_columns))
-        phase_start(sum_a.at[l], plane, send_a.at[t], recv_a.at[t])
+        phase_start(sum_a.at[l], column, send_a.at[t], recv_a.at[t])
         for copy in grad_copies(l):
             copy.start()
 
         @pl.when(l == 2)
         def _():
-            correlate_b(l)
+            correlate_c(l)
 
         phase_wait(sum_a.at[l], recv_a.at[t])
         sum_b[l, 0] = jnp.sum(sum_a[l], axis=0) * (1.0 / SIDE)
-        phase_start(sum_b.at[l], column, send_b.at[t], recv_b.at[t])
-
-        @pl.when(l == 2)
-        def _():
-            correlate_c(l)
+        phase_start(sum_b.at[l], plane, send_b.at[t], recv_b.at[t])
 
         expand(l)
+        if not last:
+
+            @pl.when(l == 1)
+            def _():
+                lax.fori_loop(0, 6, drain, 0)
+
         for copy in grad_copies(l):
             copy.wait_recv()
         phase_wait(sum_b.at[l], recv_b.at[t])
@@ -568,15 +573,6 @@
     lax.fori_loop(0, 2, backward, 0)
     layer(0, True)
 
-    def drain(k, carry):
-        phase_wait(buf_a.at[k], send_a.at[k])
-        phase_wait(buf_b.at[k], send_b.at[k])
-        for copy in ring_copies(k) + wide_copies(k):
-            copy.wait_send()
-        return carry
-
-    lax.fori_loop(0, 6, drain, 0)
-
     def drain_back(l, carry):
         phase_wait(sum_a.at[l], send_a.at[8 - l])
         phase_wait(sum_b.at[l], send_b.at[8 - l])
@@ -599,9 +595,10 @@
     return pl.pallas_call(
         kernel,
         out_shape=jax.ShapeDtypeStruct((H, W, C), F32),
-        in_specs=[vmem, vmem, hbm, hbm, hbm],
+        in_specs=[vmem, hbm, hbm, hbm, hbm],
         out_specs=vmem,
         scratch_shapes=[
+            pltpu.VMEM((H, W, C), BF16),
             pltpu.VMEM((FH, FW, C), BF16),
             pltpu.VMEM((7, 9, C, C), BF16),
             pltpu.VMEM((6, RT, WT, C), F32),
@@ -612,7 +609,7 @@
             pltpu.VMEM((6, RT - 2, WT, C), F32),
             pltpu.VMEM((6, 8, C), F32),
             pltpu.VMEM((RT, WB, 3 * C), BF16),
-            pltpu.VMEM((H + 2, W, 3 * 128), BF16),
+            pltpu.VMEM((H + 2, W, 3 * C), BF16),
             pltpu.VMEM((H + 1, W, 3 * C), BF16),
             pltpu.VMEM((H, W, 3 * C), BF16),
             pltpu.VMEM((6, SIDE, 4, 128), F32),
@@ -625,7 +622,7 @@
             pltpu.VMEM((3, SIDE, 2, 128), F32),
             pltpu.VMEM((32, 128), F32),
             pltpu.VMEM((2, 2 * C, 2 * C), BF16),
-            dma((8,)),
+            dma((9,)),
             dma((9,)),
             dma((9,)),
             dma((9,)),
@@ -639,8 +636,8 @@
             collective_id=0, has_side_effects=True, vmem_limit_bytes=56 * 2**20
         ),
     )(
+        pixel_mask,
         latent,
-        pixel_mask,
         cotangent,
         res_kernels.reshape(6, 9, C, C),
         up_kernel.reshape(9, C, C),

time: 137 us -> 120 us (0.88)
  Pallas kernels: 135 us -> 118 us
    pallas_call x1, Pallas kernels: 135 us -> 118 us  [per_device(): pl.pallas_call(kernel, out_shape=jax.ShapeDtypeStruct((H, W, C), F32), in...]
where the time goes in v3:
time: 120 us
  Pallas kernels  118 us (98%)
  local copies, waits for them, and re-layouts  1.87 us (2%)
    pallas_call x1, Pallas kernels, per_device(): pl.pallas_call(kernel, out_shape=jax.ShapeDtypeStruct((H, W, C), F32), in...  118 us

profile of v3, /device:TPU:1, one launch (start us, length us, event | category | flops | bytes accessed | tf_op | source)
XLA Modules:
  0.0 119.7 jit_solution(7870357911873015995)
XLA Ops:
  0.0 117.8 %shard_map.55 = f32[8,64,256]{2,1,0:T(8,128)} custom-call(s32[16,128]{1,0:T(8,128)} %mask.1, bf16[8,64,256]{2,1,0:T(8,128)(2,1)} %latent_hbm.1, bf16[16,128,256]{2,1,0:T(8,128)(2,1)} %cot_hbm.1, bf16[6,9,256,256]{3,2,1,0:T(8,128)(2,1)} %bitcast.2, bf16[9,256,256]{2,1,0:T(8,128)(2,1)} %bitcast.3), custom_call_target="tpu_custom_call" | custom-call | tf_op jit(solution)/shard_map/pallas_call | solution.py:595
  117.8 1.9 %copy.7 = f32[8,64,256]{2,1,0:T(8,128)} copy(f32[8,64,256]{2,1,0:T(8,128)} %shard_map.55) | data formatting | bytes 1048576

commit v4 on v3

--- a/solution.py
+++ b/solution.py
@@ -21,6 +21,7 @@
 FH, FW = 2 * H, 2 * W
 FWT = FW + 16
 SIDE = 16
+CHIPS = 128
 PIXELS = H * W
 GROUP = 8
 
@@ -53,6 +54,25 @@
                 far = min(dz, 8 - dz)
                 out.append((far, dz * 2 + dc, c - core + (core + dc) % 2, (r + dz) % 8))
     return [p[1:] for p in sorted(out, key=lambda p: -p[0])]
+
+
+def other_core():
+    c, r, core, x, y = position()
+    return c - core + (core + 1) % 2, r
+
+
+def chip_peers(visit):
+    c, r, core, x, y = position()
+    plane = [(0, c, r)] + plane_peers()[::-1]
+
+    def level(i, carry):
+        dz = jnp.where(i % 2 == 0, 4 + i // 2, 4 - (i + 1) // 2)
+        row = (r + dz) % 8
+        for slot, col, _ in plane[::-1]:
+            visit(dz * SIDE + slot, col, row)
+        return carry
+
+    lax.fori_loop(0, 7, level, 0)
 
 
 def neighbours():
@@ -113,18 +133,27 @@
     pltpu.make_async_copy(buf.at[pl.ds(1, SIDE - 1)], buf.at[pl.ds(1, SIDE - 1)], sem).wait()
 
 
-def merge_moments(parts, count):
-    mean = jnp.sum(parts[:, 0:2], axis=0) * (1.0 / SIDE)
-    delta = parts[:, 0:2] - mean[None]
-    square = jnp.sum(parts[:, 2:4] + delta * delta * float(count), axis=0)
-    return mean, square
-
-
 def lane_swap(value, step):
     lane = lax.broadcasted_iota(jnp.int32, value.shape, 1)
     return jnp.where((lane & step) != 0, pltpu.roll(value, step, 1), pltpu.roll(value, 128 - step, 1))
 
 
+def own_lanes():
+    lane = lax.broadcasted_iota(jnp.int32, (8, 128), 1)
+    return (lane & 7) == lax.broadcasted_iota(jnp.int32, (8, 128), 0)
+
+
+def packed(rows):
+    return jnp.sum(jnp.where(own_lanes(), rows, 0.0), axis=0, keepdims=True)
+
+
+def unpacked(row):
+    rows = jnp.where(own_lanes(), jnp.broadcast_to(row, (8, 128)), 0.0)
+    for step in (1, 2, 4):
+        rows = rows + lane_swap(rows, step)
+    return rows
+
+
 def wide(value):
     return jnp.concatenate([value[0:1], value[1:2]], axis=1).reshape(1, 1, C)
 
@@ -136,7 +165,7 @@
 def kernel(
     mask, latent_hbm, cot_hbm, res_hbm, up_hbm, out,
     latent, cot, weights, fields, grads, total, pre, fine, slopes, stats, taps, taps_n, box_a, box_b,
-    buf_a, buf_b, sum_a, sum_b, cor_own, cor_a, cor_b, cor_c, cor, expanded,
+    buf_a, buf_b, lines, means, cor_own, cor_a, cor_b, cor_c, cor, expanded,
     load_sem, send_a, send_b, recv_a, recv_b, csend, crecv, hsend, hrecv,
 ):
     c, r, _, px, py = position()
@@ -157,9 +186,14 @@
     latent_copy.start()
     barrier = pltpu.get_barrier_semaphore()
     plane, column = plane_peers(), column_peers()
-    greeted = [p[1:] for p in plane] + [p[1:] for p in column] + [p[2:] for p in neighbours()]
-    for col, row in greeted:
+
+    def greet(slot, col, row):
         pl.semaphore_signal(barrier, inc=1, device_id={"cols": col, "rows": row}, device_id_type=MESH)
+
+    chip_peers(greet)
+    greeted = plane + column + [(0,) + p[2:] for p in neighbours()]
+    for peer in greeted:
+        greet(*peer)
 
     cot_copy.start()
     weight_copy(0).start()
@@ -186,12 +220,69 @@
         mean = jnp.sum(x, axis=(0, 1)).reshape(1, C) * (1.0 / PIXELS)
         delta = x - mean.reshape(1, 1, C)
         square = jnp.sum(delta * delta, axis=(0, 1)).reshape(1, C)
-        put_rows(buf_a.at[k, 0], 0, mean, square)
-
-    def put_sums(l, at, d, n):
+        means[k, 0:1, :] = mean
+        put_rows(lines, 0, mean, square)
+        mean, square = lines[0:2], lines[2:4]
+        count = float(PIXELS)
+        for step in (1, 2, 4):
+            other, squares = lane_swap(mean, step), lane_swap(square, step)
+            delta = mean - other
+            mean = (mean + other) * 0.5
+            square = square + squares + delta * delta * (count * 0.5)
+            count *= 2.0
+        lines[0:2] = mean
+        lines[2:4] = square
+        lines[4:8] = jnp.zeros((4, 128), F32)
+        buf_a[k, 0:1, :] = packed(lines[...])
+
+    def put_sums(at, d, n):
         first = jnp.sum(d, axis=(0, 1)).reshape(1, C) * (1.0 / PIXELS)
         second = jnp.sum(d * n, axis=(0, 1)).reshape(1, C) * (1.0 / PIXELS)
-        put_rows(sum_a.at[l, 0], at, first, second)
+        put_rows(lines, at, first, second)
+
+    def pack_sums(t):
+        rows = lines[...]
+        for step in (1, 2, 4):
+            rows = rows + lane_swap(rows, step)
+        buf_a[t, 0:1, :] = packed(rows * (1.0 / GROUP))
+
+    def send_all(t, first, then):
+        def send(slot, col, row):
+            pltpu.make_async_remote_copy(
+                src_ref=buf_a.at[t, pl.ds(0, 1)],
+                dst_ref=buf_a.at[t, pl.ds(slot, 1)],
+                send_sem=send_a.at[t],
+                recv_sem=recv_a.at[t],
+                device_id={"cols": col, "rows": row},
+                device_id_type=MESH,
+            ).start()
+
+        chip_peers(send)
+        for copy in first:
+            copy.start()
+        for peer in plane:
+            send(*peer)
+        for copy in then:
+            copy.start()
+
+    def wait_all(t, sem):
+        part = buf_a.at[t, pl.ds(1, CHIPS - 1)]
+        pltpu.make_async_copy(part, part, sem.at[t]).wait()
+
+    def core_copy(t):
+        col, row = other_core()
+        return pltpu.make_async_remote_copy(
+            src_ref=buf_b.at[t, 0],
+            dst_ref=buf_b.at[t, 1],
+            send_sem=send_b.at[t],
+            recv_sem=recv_b.at[t],
+            device_id={"cols": col, "rows": row},
+            device_id_type=MESH,
+        )
+
+    def swap_cores(t, row):
+        buf_b[t, 0] = jnp.broadcast_to(row, (8, 128))
+        core_copy(t).start()
 
     def ring_copies(k):
         return halo_copies(fields.at[k], T, H, W, WT, (1, 1), (1, 3), hsend.at[k], hrecv.at[k])
@@ -254,11 +345,9 @@
     put_moments(0, latent[...].astype(F32))
 
     def start_a(k):
-        phase_start(buf_a.at[k], column, send_a.at[k], recv_a.at[k])
-        for copy in ring_copies(k) + wide_copies(k):
-            copy.start()
-
-    pl.semaphore_wait(barrier, len(greeted))
+        send_all(k, ring_copies(k), wide_copies(k))
+
+    pl.semaphore_wait(barrier, CHIPS - SIDE + len(greeted))
     start_a(0)
     cot_copy.wait()
 
@@ -323,7 +412,7 @@
 
     def correlate(l):
         k = 2 * l
-        mean = jnp.concatenate([buf_a[k + 1, 0, 0:1, :], buf_a[k + 1, 0, 1:2, :]], axis=1)
+        mean = means[k + 1, 0:1, :]
 
         def plain_slope(first, rows):
             return slopes[k, first - 1 : first - 1 + rows]
@@ -409,16 +498,24 @@
                 block = lax.dot_general(spread, block, (((0,), (0,)), ((), ())), preferred_element_type=F32)
                 expanded[part, j * C : (j + 1) * C, :] = block.astype(BF16)
 
+    lane = lax.broadcasted_iota(jnp.int32, (1, 128), 1) & 7
+
+    def chips_moments(k):
+        parts = buf_a[k]
+        total_row = jnp.sum(parts, axis=0, keepdims=True)
+        mean = total_row * (1.0 / CHIPS)
+        delta = parts - mean
+        square = jnp.sum(delta * delta, axis=0, keepdims=True) * float(PIXELS * GROUP)
+        return jnp.where(lane < 2, mean, jnp.where(lane < 4, total_row + pltpu.roll(square, 2, 1), 0.0))
+
     def finish_moments(k):
-        mean, square = merge_moments(buf_b[k], PIXELS * SIDE)
-        count = float(PIXELS * SIDE * SIDE)
-        for step in (1, 2, 4):
-            other, squares = lane_swap(mean, step), lane_swap(square, step)
-            delta = mean - other
-            mean = (mean + other) * 0.5
-            square = square + squares + delta * delta * (count * 0.5)
-            count *= 2.0
-        inv = lax.rsqrt(square * (1.0 / count) + EPS)
+        mine, theirs = buf_b[k, 0, 0:1], buf_b[k, 1, 0:1]
+        delta = mine - theirs
+        square = delta * delta * float(PIXELS * GROUP * CHIPS // 2)
+        both = jnp.where(lane < 2, (mine + theirs) * 0.5, mine + theirs + pltpu.roll(square, 2, 1))
+        rows = unpacked(both)
+        mean = rows[0:2]
+        inv = lax.rsqrt(rows[2:4] * (1.0 / (PIXELS * GROUP * CHIPS * 2)) + EPS)
         mean, inv = wide(mean), wide(inv)
         stats[k, 0:1, :] = mean.reshape(1, C)
         stats[k, 1:2, :] = inv.reshape(1, C)
@@ -428,7 +525,13 @@
         @pl.when(k > 0)
         def _():
             start_a(k)
+            for copy in wide_copies(k - 1)[0::3]:
+                copy.wait_recv()
             slope(k - 1, 1, RT - 1)
+
+        @pl.when((k == 3) | (k == 5))
+        def _():
+            correlate_c(k // 2 - 1)
 
         @pl.when(k % 2 == 1)
         def _():
@@ -436,17 +539,7 @@
 
         @pl.when((k == 2) | (k == 4))
         def _():
-            correlate_c(k // 2 - 1)
-
-        phase_wait(buf_a.at[k], recv_a.at[k])
-        mean, square = merge_moments(buf_a[k], PIXELS)
-        buf_b[k, 0, 0:2, :] = mean
-        buf_b[k, 0, 2:4, :] = square
-        phase_start(buf_b.at[k], plane, send_b.at[k], recv_b.at[k])
-
-        @pl.when(k % 2 == 1)
-        def _():
-            correlate_b(k // 2)
+            correlate_b(k // 2 - 1)
 
         @pl.when(k == 2)
         def _():
@@ -464,9 +557,11 @@
         def _():
             weight_copy(k).wait()
 
-        for copy in ring_copies(k) + wide_copies(k):
+        wait_all(k, recv_a)
+        swap_cores(k, chips_moments(k))
+        for copy in ring_copies(k) + wide_copies(k)[1:3]:
             copy.wait_recv()
-        phase_wait(buf_b.at[k], recv_b.at[k])
+        core_copy(k).wait_recv()
         mean, inv = finish_moments(k)
 
         @pl.when(k < 5)
@@ -488,8 +583,8 @@
     slope(5, T - 1, T + H + 1)
 
     def drain(k, carry):
-        phase_wait(buf_a.at[k], send_a.at[k])
-        phase_wait(buf_b.at[k], send_b.at[k])
+        wait_all(k, send_a)
+        core_copy(k).wait_send()
         for copy in ring_copies(k) + wide_copies(k):
             copy.wait_send()
         return carry
@@ -502,7 +597,7 @@
         grads[l, tile_rows, tile_columns, :] = (
             pre[1 : H + 1, 0:W] * slopes[k + 1, T - 1 : T - 1 + H, 0:W]
         )
-        put_sums(l, 0, grads[l, tile_rows, tile_columns, :], normed(k + 1, tile_rows, tile_columns))
+        put_sums(0, grads[l, tile_rows, tile_columns, :], normed(k + 1, tile_rows, tile_columns))
 
         def unprojected(first, rows):
             at = first - T + 1
@@ -510,32 +605,38 @@
 
         put_taps(unprojected, T - 1, T + H + 1, W)
         d = tap_conv_back(k, H, W) * slopes[k, T - 1 : T - 1 + H, 0:W]
-        put_sums(l, 4, d, normed(k, tile_rows, tile_columns))
-        phase_start(sum_a.at[l], column, send_a.at[t], recv_a.at[t])
-        for copy in grad_copies(l):
-            copy.start()
-
-        @pl.when(l == 2)
-        def _():
-            correlate_c(l)
-
-        phase_wait(sum_a.at[l], recv_a.at[t])
-        sum_b[l, 0] = jnp.sum(sum_a[l], axis=0) * (1.0 / SIDE)
-        phase_start(sum_b.at[l], plane, send_b.at[t], recv_b.at[t])
-
-        expand(l)
-        if not last:
+        put_sums(4, d, normed(k, tile_rows, tile_columns))
+        pack_sums(t)
+        send_all(t, grad_copies(l), [])
+
+        if last:
+            expand(l)
+        else:
+
+            @pl.when(l == 2)
+            def _():
+                correlate_b(l)
+                for copy in wide_copies(5)[0::3]:
+                    copy.wait_recv()
 
             @pl.when(l == 1)
             def _():
+                expand(l)
                 lax.fori_loop(0, 6, drain, 0)
+
+        wait_all(t, recv_a)
+        swap_cores(t, jnp.sum(buf_a[t], axis=0, keepdims=True) * (1.0 / CHIPS))
+        if not last:
+
+            @pl.when(l == 2)
+            def _():
+                correlate_c(l)
+                expand(l)
 
         for copy in grad_copies(l):
             copy.wait_recv()
-        phase_wait(sum_b.at[l], recv_b.at[t])
-        sums = jnp.sum(sum_b[l], axis=0) * (1.0 / (SIDE * GROUP))
-        for step in (1, 2, 4):
-            sums = sums + lane_swap(sums, step)
+        core_copy(t).wait_recv()
+        sums = unpacked((buf_b[t, 0, 0:1] + buf_b[t, 1, 0:1]) * 0.5)
         first2, second2, first1, second1 = (wide(sums[i : i + 2]) for i in (0, 2, 4, 6))
         scaled = inv2 * second2
         source = jnp.concatenate([inv2 * scaled, inv2 * (first2 - mean2 * scaled)], axis=-1).reshape(1, 2 * C)
@@ -574,8 +675,8 @@
     layer(0, True)
 
     def drain_back(l, carry):
-        phase_wait(sum_a.at[l], send_a.at[8 - l])
-        phase_wait(sum_b.at[l], send_b.at[8 - l])
+        wait_all(8 - l, send_a)
+        core_copy(8 - l).wait_send()
         phase_wait(cor_a.at[l], csend.at[l])
         phase_wait(cor_b.at[l], csend.at[l + 3])
         phase_wait(cor_c.at[l], csend.at[l + 6])
@@ -612,10 +713,10 @@
             pltpu.VMEM((H + 2, W, 3 * C), BF16),
             pltpu.VMEM((H + 1, W, 3 * C), BF16),
             pltpu.VMEM((H, W, 3 * C), BF16),
-            pltpu.VMEM((6, SIDE, 4, 128), F32),
-            pltpu.VMEM((6, SIDE, 4, 128), F32),
-            pltpu.VMEM((3, SIDE, 8, 128), F32),
-            pltpu.VMEM((3, SIDE, 8, 128), F32),
+            pltpu.VMEM((9, CHIPS, 128), F32),
+            pltpu.VMEM((9, 2, 8, 128), F32),
+            pltpu.VMEM((8, 128), F32),
+            pltpu.VMEM((6, 8, C), F32),
             pltpu.VMEM((3, SIDE, 2, 128), F32),
             pltpu.VMEM((3, SIDE, 2, 128), F32),
             pltpu.VMEM((3, SIDE, 2, 128), F32),

time: 120 us -> 120 us (level)
  no operation moved by 1% of the time
where the time goes in v4:
time: 120 us
  Pallas kernels  118 us (98%)
  local copies, waits for them, and re-layouts  1.87 us (2%)
    pallas_call x1, Pallas kernels, per_device(): pl.pallas_call(kernel, out_shape=jax.ShapeDtypeStruct((H, W, C), F32), in...  118 us

profile of v4, /device:TPU:1, one launch (start us, length us, event | category | flops | bytes accessed | tf_op | source)
XLA Modules:
  0.0 119.8 jit_solution(466252049128360075)
XLA Ops:
  0.0 117.9 %shard_map.55 = f32[8,64,256]{2,1,0:T(8,128)} custom-call(s32[16,128]{1,0:T(8,128)} %mask.1, bf16[8,64,256]{2,1,0:T(8,128)(2,1)} %latent_hbm.1, bf16[16,128,256]{2,1,0:T(8,128)(2,1)} %cot_hbm.1, bf16[6,9,256,256]{3,2,1,0:T(8,128)(2,1)} %bitcast.2, bf16[9,256,256]{2,1,0:T(8,128)(2,1)} %bitcast.3), custom_call_target="tpu_custom_call" | custom-call | tf_op jit(solution)/shard_map/pallas_call | solution.py:696
  117.9 1.9 %copy.7 = f32[8,64,256]{2,1,0:T(8,128)} copy(f32[8,64,256]{2,1,0:T(8,128)} %shard_map.55) | data formatting | bytes 1048576

commit v5 on v4

--- a/solution.py
+++ b/solution.py
@@ -85,7 +85,7 @@
     return out
 
 
-def halo_copies(field, top, height, width, total, edges, corners, send, recv):
+def halo_copies(field, rows, columns, corners, send, recv, top=T, height=H, width=W, total=WT):
     def spans(step, first, size, end, near, far):
         n = far - near + 1
         if step < 0:
@@ -96,7 +96,7 @@
 
     copies = []
     for dr, dc, col, row in neighbours():
-        band = corners if dr and dc else edges
+        band = corners if dr and dc else (rows if dr else columns)
         if band is None:
             continue
         src_r, dst_r = spans(dr, top, height, top, *band)
@@ -164,7 +164,7 @@
 
 def kernel(
     mask, latent_hbm, cot_hbm, res_hbm, up_hbm, out,
-    latent, cot, weights, fields, grads, total, pre, fine, slopes, stats, taps, taps_n, box_a, box_b,
+    latent, cot, weights, fields, grads, grads_out, grads_in, total, pre, fine, rows_out, rows_in, slopes, stats, taps, taps_n, box_a, box_b,
     buf_a, buf_b, lines, means, cor_own, cor_a, cor_b, cor_c, cor, expanded,
     load_sem, send_a, send_b, recv_a, recv_b, csend, crecv, hsend, hrecv,
 ):
@@ -285,19 +285,52 @@
         core_copy(t).start()
 
     def ring_copies(k):
-        return halo_copies(fields.at[k], T, H, W, WT, (1, 1), (1, 3), hsend.at[k], hrecv.at[k])
+        return halo_copies(fields.at[k], (1, 1), (1, 3), (1, 3), hsend.at[k], hrecv.at[k])
 
     def wide_copies(k):
-        return halo_copies(fields.at[k], T, H, W, WT, (2, 3), None, hsend.at[k + 6], hrecv.at[k + 6])
-
-    def grad_copies(l):
-        return halo_copies(grads.at[l], T, H, W, WT, (1, 3), (1, 3), hsend.at[l + 12], hrecv.at[l + 12])
+        return halo_copies(fields.at[k], (2, 3), None, None, hsend.at[k + 6], hrecv.at[k + 6])
+
+    def grad_copies(l, last):
+        far = 1 if last else 3
+        copies = halo_copies(grads.at[l], None, (1, far), (1, far), hsend.at[l + 12], hrecv.at[l + 12])
+        c, r, _, _, _ = position()
+        for i, (first, dst_first) in enumerate(((0, 0), (H - far, 3 - far))):
+            copies.append(
+                pltpu.make_async_remote_copy(
+                    src_ref=grads_out.at[l, pl.ds(first, far)],
+                    dst_ref=grads_in.at[l, 1 - i, pl.ds(dst_first, far)],
+                    send_sem=hsend.at[l + 12, 6 + i],
+                    recv_sem=hrecv.at[l + 12, 6 + i],
+                    device_id={"cols": c, "rows": (r + 2 * i + 7) % 8},
+                    device_id_type=MESH,
+                )
+            )
+        return copies
 
     def total_copies():
-        return halo_copies(total, T, H, W, WT, (1, 2), (1, 2), hsend.at[15], hrecv.at[15])
+        return halo_copies(total, (1, 2), (1, 2), (1, 2), hsend.at[15], hrecv.at[15])
 
     def fine_copies():
-        return halo_copies(fine, 1, FH, FW, FWT, (1, 1), (1, 1), hsend.at[16], hrecv.at[16])
+        copies = []
+        for i, (dr, dc, col, row) in enumerate(neighbours()):
+            if dc == 0:
+                src, dst = rows_out.at[max(dr, 0)], rows_in.at[max(-dr, 0)]
+            else:
+                src_r = pl.ds(1, FH) if dr == 0 else (pl.ds(1, 1) if dr < 0 else pl.ds(FH, 1))
+                dst_r = pl.ds(1, FH) if dr == 0 else (pl.ds(FH + 1, 1) if dr < 0 else pl.ds(0, 1))
+                src = fine.at[:, src_r, pl.ds(0 if dc < 0 else FW - 1, 1), :]
+                dst = fine.at[:, dst_r, pl.ds(FW if dc < 0 else FWT - 1, 1), :]
+            copies.append(
+                pltpu.make_async_remote_copy(
+                    src_ref=src,
+                    dst_ref=dst,
+                    send_sem=hsend.at[16, i],
+                    recv_sem=hrecv.at[16, i],
+                    device_id={"cols": col, "rows": row},
+                    device_id_type=MESH,
+                )
+            )
+        return copies
 
     def put_taps(make, first, last, columns, dst=taps):
         parts = ((first, T, top), (T, T + H, None), (T + H, last, bottom))
@@ -348,7 +381,7 @@
         send_all(k, ring_copies(k), wide_copies(k))
 
     pl.semaphore_wait(barrier, CHIPS - SIDE + len(greeted))
-    start_a(0)
+    send_all(0, ring_copies(0), wide_copies(0))
     cot_copy.wait()
 
     def mask_row(i, carry):
@@ -358,6 +391,8 @@
         return carry
 
     lax.fori_loop(0, FH, mask_row, 0)
+    for i, at in enumerate((1, FH)):
+        rows_out[i] = jnp.concatenate([fine[0, at, 0:FW, :], fine[1, at, 0:FW, :]], axis=1).astype(BF16)
     for copy in fine_copies():
         copy.start()
 
@@ -369,8 +404,11 @@
     def boxes():
         for copy in fine_copies():
             copy.wait_recv()
-        fine[:, 0] = fine[:, 0] * top
-        fine[:, FH + 1] = fine[:, FH + 1] * bottom
+        for i, (at, scale) in enumerate(((0, top), (FH + 1, bottom))):
+            edge_row = rows_in[i].astype(F32) * scale
+            fine[0, at, 0:FW, :] = edge_row[:, 0:128]
+            fine[1, at, 0:FW, :] = edge_row[:, 128:256]
+            fine[:, at, FW:FWT, :] = fine[:, at, FW:FWT, :] * scale
         fine[:, :, FW : FW + 8, :] = fine[:, :, FW : FW + 8, :] * right
         fine[:, :, FWT - 8 : FWT, :] = fine[:, :, FWT - 8 : FWT, :] * left
 
@@ -525,7 +563,7 @@
         @pl.when(k > 0)
         def _():
             start_a(k)
-            for copy in wide_copies(k - 1)[0::3]:
+            for copy in wide_copies(k - 1):
                 copy.wait_recv()
             slope(k - 1, 1, RT - 1)
 
@@ -559,7 +597,7 @@
 
         wait_all(k, recv_a)
         swap_cores(k, chips_moments(k))
-        for copy in ring_copies(k) + wide_copies(k)[1:3]:
+        for copy in ring_copies(k):
             copy.wait_recv()
         core_copy(k).wait_recv()
         mean, inv = finish_moments(k)
@@ -597,6 +635,7 @@
         grads[l, tile_rows, tile_columns, :] = (
             pre[1 : H + 1, 0:W] * slopes[k + 1, T - 1 : T - 1 + H, 0:W]
         )
+        grads_out[l] = grads[l, tile_rows, tile_columns, :].astype(BF16)
         put_sums(0, grads[l, tile_rows, tile_columns, :], normed(k + 1, tile_rows, tile_columns))
 
         def unprojected(first, rows):
@@ -607,7 +646,7 @@
         d = tap_conv_back(k, H, W) * slopes[k, T - 1 : T - 1 + H, 0:W]
         put_sums(4, d, normed(k, tile_rows, tile_columns))
         pack_sums(t)
-        send_all(t, grad_copies(l), [])
+        send_all(t, grad_copies(l, last), [])
 
         if last:
             expand(l)
@@ -616,7 +655,7 @@
             @pl.when(l == 2)
             def _():
                 correlate_b(l)
-                for copy in wide_copies(5)[0::3]:
+                for copy in wide_copies(5):
                     copy.wait_recv()
 
             @pl.when(l == 1)
@@ -631,25 +670,29 @@
             @pl.when(l == 2)
             def _():
                 correlate_c(l)
-                expand(l)
-
-        for copy in grad_copies(l):
+
+        for copy in grad_copies(l, last):
             copy.wait_recv()
+        far = 1 if last else 3
+        grads[l, T - far : T, tile_columns, :] = grads_in[l, 0, 3 - far : 3].astype(F32)
+        grads[l, T + H : T + H + far, tile_columns, :] = grads_in[l, 1, 0:far].astype(F32)
         core_copy(t).wait_recv()
         sums = unpacked((buf_b[t, 0, 0:1] + buf_b[t, 1, 0:1]) * 0.5)
-        first2, second2, first1, second1 = (wide(sums[i : i + 2]) for i in (0, 2, 4, 6))
-        scaled = inv2 * second2
-        source = jnp.concatenate([inv2 * scaled, inv2 * (first2 - mean2 * scaled)], axis=-1).reshape(1, 2 * C)
-        source = jnp.broadcast_to(source * (1.0 / GROUP), (16, 2 * C))
-        high = source.astype(BF16)
-        low = (source - high.astype(F32)).astype(BF16)
-        moved = (
-            jnp.dot(high, expanded[0], preferred_element_type=F32)
-            + jnp.dot(low, expanded[0], preferred_element_type=F32)
-            + jnp.dot(high, expanded[1], preferred_element_type=F32)
-        )
-        first1 = first1 - moved[0:1, 0:C].reshape(1, 1, C)
-        second1 = second1 - moved[0:1, C : 2 * C].reshape(1, 1, C)
+        first2, second2, first1_raw, second1_raw = (wide(sums[i : i + 2]) for i in (0, 2, 4, 6))
+        def second_sums():
+            scaled = inv2 * second2
+            source = jnp.concatenate([inv2 * scaled, inv2 * (first2 - mean2 * scaled)], axis=-1).reshape(1, 2 * C)
+            source = jnp.broadcast_to(source * (1.0 / GROUP), (16, 2 * C))
+            high = source.astype(BF16)
+            low = (source - high.astype(F32)).astype(BF16)
+            moved = (
+                jnp.dot(high, expanded[0], preferred_element_type=F32)
+                + jnp.dot(low, expanded[0], preferred_element_type=F32)
+                + jnp.dot(high, expanded[1], preferred_element_type=F32)
+            )
+            first1_left = first1_raw - moved[0:1, 0:C].reshape(1, 1, C)
+            second1_left = second1_raw - moved[0:1, C : 2 * C].reshape(1, 1, C)
+            return first1_left, second1_left
 
         def back(first, rows):
             at = slice(first, first + rows)
@@ -659,11 +702,18 @@
             put_taps(back, T - 1, T + H + 1, W)
             d = tap_conv_back(k, H, W) * slopes[k, T - 1 : T - 1 + H, 0:W]
             n = normed(k, tile_rows, tile_columns)
+            first1, second1 = second_sums()
             out[...] = total[tile_rows, tile_columns, :] + inv1 * (d - first1 - n * second1)
         else:
             put_taps(back, 0, RT, WB)
             d = tap_conv_back(k, H + 4, WB)[:, 0:WT] * slopes[k]
             rows = slice(T - 2, T + H + 2)
+
+            @pl.when(l == 2)
+            def _():
+                expand(l)
+
+            first1, second1 = second_sums()
             total[rows] += inv1 * (d - first1 - normed(k, rows) * second1)
             lift(k - 1)
 
@@ -674,17 +724,14 @@
     lax.fori_loop(0, 2, backward, 0)
     layer(0, True)
 
-    def drain_back(l, carry):
+    for l in range(3):
         wait_all(8 - l, send_a)
         core_copy(8 - l).wait_send()
         phase_wait(cor_a.at[l], csend.at[l])
         phase_wait(cor_b.at[l], csend.at[l + 3])
         phase_wait(cor_c.at[l], csend.at[l + 6])
-        for copy in grad_copies(l):
+        for copy in grad_copies(l, l == 0):
             copy.wait_send()
-        return carry
-
-    lax.fori_loop(0, 3, drain_back, 0)
     for copy in fine_copies():
         copy.wait_send()
 
@@ -704,9 +751,13 @@
             pltpu.VMEM((7, 9, C, C), BF16),
             pltpu.VMEM((6, RT, WT, C), F32),
             pltpu.VMEM((3, RT, WT, C), F32),
+            pltpu.VMEM((3, H, W, C), BF16),
+            pltpu.VMEM((3, 2, 3, W, C), BF16),
             pltpu.VMEM((RT, WT, C), F32),
             pltpu.VMEM((H + 2, WT, C), F32),
             pltpu.VMEM((2, FH + 2, FWT, 128), F32),
+            pltpu.VMEM((2, FW, C), BF16),
+            pltpu.VMEM((2, FW, C), BF16),
             pltpu.VMEM((6, RT - 2, WT, C), F32),
             pltpu.VMEM((6, 8, C), F32),
             pltpu.VMEM((RT, WB, 3 * C), BF16),

time: 120 us -> 115 us (0.958)
  Pallas kernels: 118 us -> 113 us
    pallas_call x1, Pallas kernels: 118 us -> 113 us  [per_device(): pl.pallas_call(kernel, out_shape=jax.ShapeDtypeStruct((H, W, C), F32), in...]
where the time goes in v5:
time: 115 us
  Pallas kernels  113 us (98%)
  local copies, waits for them, and re-layouts  1.87 us (2%)
    pallas_call x1, Pallas kernels, per_device(): pl.pallas_call(kernel, out_shape=jax.ShapeDtypeStruct((H, W, C), F32), in...  113 us

profile of v5, /device:TPU:1, one launch (start us, length us, event | category | flops | bytes accessed | tf_op | source)
XLA Modules:
  0.0 114.5 jit_solution(10452712987593819902)
XLA Ops:
  0.0 112.6 %shard_map.55 = f32[8,64,256]{2,1,0:T(8,128)} custom-call(s32[16,128]{1,0:T(8,128)} %mask.1, bf16[8,64,256]{2,1,0:T(8,128)(2,1)} %latent_hbm.1, bf16[16,128,256]{2,1,0:T(8,128)(2,1)} %cot_hbm.1, bf16[6,9,256,256]{3,2,1,0:T(8,128)(2,1)} %bitcast.2, bf16[9,256,256]{2,1,0:T(8,128)(2,1)} %bitcast.3), custom_call_target="tpu_custom_call" | custom-call | tf_op jit(solution)/shard_map/pallas_call | solution.py:743
  112.6 1.9 %copy.7 = f32[8,64,256]{2,1,0:T(8,128)} copy(f32[8,64,256]{2,1,0:T(8,128)} %shard_map.55) | data formatting | bytes 1048576

commit v6 on v5

--- a/solution.py
+++ b/solution.py
@@ -21,7 +21,8 @@
 FH, FW = 2 * H, 2 * W
 FWT = FW + 16
 SIDE = 16
-CHIPS = 128
+HALF = 64
+OWN = 3 * SIDE
 PIXELS = H * W
 GROUP = 8
 
@@ -63,16 +64,27 @@
 
 def chip_peers(visit):
     c, r, core, x, y = position()
-    plane = [(0, c, r)] + plane_peers()[::-1]
-
-    def level(i, carry):
-        dz = jnp.where(i % 2 == 0, 4 + i // 2, 4 - (i + 1) // 2)
-        row = (r + dz) % 8
-        for slot, col, _ in plane[::-1]:
-            visit(dz * SIDE + slot, col, row)
+    plane = plane_peers()
+
+    def level(i):
+        even = jnp.where(i == 0, 4, jnp.where(i == 1, 2, jnp.where(i == 2, 6, 0)))
+        odd = jnp.where(i == 0, 3, jnp.where(i == 1, 5, jnp.where(i == 2, 1, 7)))
+        row = (r + jnp.where(core == 0, even, odd)) % 8
+        for slot, col, _ in plane:
+            visit(i * SIDE + slot, col, row)
+        return row
+
+    def whole_level(i, carry):
+        row = level(i)
+        visit(i * SIDE, c, row)
         return carry
 
-    lax.fori_loop(0, 7, level, 0)
+    lax.fori_loop(0, 3, whole_level, 0)
+    row = level(3)
+
+    @pl.when(core == 1)
+    def _():
+        visit(OWN, c, row)
 
 
 def neighbours():
@@ -165,10 +177,10 @@
 def kernel(
     mask, latent_hbm, cot_hbm, res_hbm, up_hbm, out,
     latent, cot, weights, fields, grads, grads_out, grads_in, total, pre, fine, rows_out, rows_in, slopes, stats, taps, taps_n, box_a, box_b,
-    buf_a, buf_b, lines, means, cor_own, cor_a, cor_b, cor_c, cor, expanded,
-    load_sem, send_a, send_b, recv_a, recv_b, csend, crecv, hsend, hrecv,
+    buf_a, buf_b, pair, joint, lines, means, cor_own, cor_a, cor_b, cor_c, cor, expanded,
+    load_sem, send_a, send_b, recv_a, recv_b, send_p, recv_p, csend, crecv, hsend, hrecv,
 ):
-    c, r, _, px, py = position()
+    c, r, core, px, py = position()
     place = py * 4 + px
     top = jnp.where(r == 0, 0.0, 1.0).astype(F32)
     bottom = jnp.where(r == 7, 0.0, 1.0).astype(F32)
@@ -216,7 +228,7 @@
         buf[at + 2 : at + 3, :] = second[:, 0:128]
         buf[at + 3 : at + 4, :] = second[:, 128:256]
 
-    def put_moments(k, x):
+    def moments(k, x):
         mean = jnp.sum(x, axis=(0, 1)).reshape(1, C) * (1.0 / PIXELS)
         delta = x - mean.reshape(1, 1, C)
         square = jnp.sum(delta * delta, axis=(0, 1)).reshape(1, C)
@@ -233,7 +245,10 @@
         lines[0:2] = mean
         lines[2:4] = square
         lines[4:8] = jnp.zeros((4, 128), F32)
-        buf_a[k, 0:1, :] = packed(lines[...])
+        return packed(lines[...])
+
+    def put_moments(k, x):
+        swap_cores(pair, k, moments(k, x), send_p, recv_p)
 
     def put_sums(at, d, n):
         first = jnp.sum(d, axis=(0, 1)).reshape(1, C) * (1.0 / PIXELS)
@@ -244,12 +259,14 @@
         rows = lines[...]
         for step in (1, 2, 4):
             rows = rows + lane_swap(rows, step)
-        buf_a[t, 0:1, :] = packed(rows * (1.0 / GROUP))
-
-    def send_all(t, first, then):
+        swap_cores(pair, t, packed(rows * (1.0 / GROUP)), send_p, recv_p)
+
+    def send_all(t, row, then):
+        joint[t] = jnp.broadcast_to(row, (8, 128))
+
         def send(slot, col, row):
             pltpu.make_async_remote_copy(
-                src_ref=buf_a.at[t, pl.ds(0, 1)],
+                src_ref=joint.at[t, pl.ds(0, 1)],
                 dst_ref=buf_a.at[t, pl.ds(slot, 1)],
                 send_sem=send_a.at[t],
                 recv_sem=recv_a.at[t],
@@ -258,31 +275,50 @@
             ).start()
 
         chip_peers(send)
-        for copy in first:
-            copy.start()
-        for peer in plane:
-            send(*peer)
         for copy in then:
             copy.start()
 
+        @pl.when(core == 0)
+        def _():
+            buf_a[t, OWN : OWN + 1, :] = joint[t, 0:1]
+
     def wait_all(t, sem):
-        part = buf_a.at[t, pl.ds(1, CHIPS - 1)]
-        pltpu.make_async_copy(part, part, sem.at[t]).wait()
-
-    def core_copy(t):
+        for which, count in ((0, HALF - 1), (1, HALF)):
+
+            @pl.when(core == which)
+            def _():
+                part = buf_a.at[t, pl.ds(0, count)]
+                pltpu.make_async_copy(part, part, sem.at[t]).wait()
+
+    def core_copy(buf, t, send, recv):
         col, row = other_core()
         return pltpu.make_async_remote_copy(
-            src_ref=buf_b.at[t, 0],
-            dst_ref=buf_b.at[t, 1],
-            send_sem=send_b.at[t],
-            recv_sem=recv_b.at[t],
+            src_ref=buf.at[t, 0],
+            dst_ref=buf.at[t, 1],
+            send_sem=send.at[t],
+            recv_sem=recv.at[t],
             device_id={"cols": col, "rows": row},
             device_id_type=MESH,
         )
 
-    def swap_cores(t, row):
-        buf_b[t, 0] = jnp.broadcast_to(row, (8, 128))
-        core_copy(t).start()
+    def swap_cores(buf, t, row, send, recv):
+        buf[t, 0] = jnp.broadcast_to(row, (8, 128))
+        core_copy(buf, t, send, recv).start()
+
+    def swapped(buf, t, send, recv):
+        core_copy(buf, t, send, recv).wait_recv()
+        return buf[t, 0, 0:1], buf[t, 1, 0:1]
+
+    lane = lax.broadcasted_iota(jnp.int32, (1, 128), 1) & 7
+
+    def join_moments(parts, count):
+        mine, theirs = parts
+        delta = mine - theirs
+        square = delta * delta * (count * 0.5)
+        return jnp.where(lane < 2, (mine + theirs) * 0.5, mine + theirs + pltpu.roll(square, 2, 1))
+
+    def join_means(parts):
+        return (parts[0] + parts[1]) * 0.5
 
     def ring_copies(k):
         return halo_copies(fields.at[k], (1, 1), (1, 3), (1, 3), hsend.at[k], hrecv.at[k])
@@ -375,13 +411,15 @@
 
     latent_copy.wait()
     fields[0, tile_rows, tile_columns, :] = latent[...].astype(F32)
-    put_moments(0, latent[...].astype(F32))
+    first_row = moments(0, latent[...].astype(F32))
 
     def start_a(k):
-        send_all(k, ring_copies(k), wide_copies(k))
-
-    pl.semaphore_wait(barrier, CHIPS - SIDE + len(greeted))
-    send_all(0, ring_copies(0), wide_copies(0))
+        row = join_moments(swapped(pair, k, send_p, recv_p), float(PIXELS * GROUP))
+        send_all(k, row, ring_copies(k) + wide_copies(k))
+
+    pl.semaphore_wait(barrier, HALF - 1 + core + len(greeted))
+    swap_cores(pair, 0, first_row, send_p, recv_p)
+    start_a(0)
     cot_copy.wait()
 
     def mask_row(i, carry):
@@ -536,24 +574,19 @@
                 block = lax.dot_general(spread, block, (((0,), (0,)), ((), ())), preferred_element_type=F32)
                 expanded[part, j * C : (j + 1) * C, :] = block.astype(BF16)
 
-    lane = lax.broadcasted_iota(jnp.int32, (1, 128), 1) & 7
-
     def chips_moments(k):
         parts = buf_a[k]
         total_row = jnp.sum(parts, axis=0, keepdims=True)
-        mean = total_row * (1.0 / CHIPS)
+        mean = total_row * (1.0 / HALF)
         delta = parts - mean
-        square = jnp.sum(delta * delta, axis=0, keepdims=True) * float(PIXELS * GROUP)
+        square = jnp.sum(delta * delta, axis=0, keepdims=True) * float(PIXELS * GROUP * 2)
         return jnp.where(lane < 2, mean, jnp.where(lane < 4, total_row + pltpu.roll(square, 2, 1), 0.0))
 
     def finish_moments(k):
-        mine, theirs = buf_b[k, 0, 0:1], buf_b[k, 1, 0:1]
-        delta = mine - theirs
-        square = delta * delta * float(PIXELS * GROUP * CHIPS // 2)
-        both = jnp.where(lane < 2, (mine + theirs) * 0.5, mine + theirs + pltpu.roll(square, 2, 1))
+        both = join_moments(swapped(buf_b, k, send_b, recv_b), float(PIXELS * GROUP * 2 * HALF))
         rows = unpacked(both)
         mean = rows[0:2]
-        inv = lax.rsqrt(rows[2:4] * (1.0 / (PIXELS * GROUP * CHIPS * 2)) + EPS)
+        inv = lax.rsqrt(rows[2:4] * (1.0 / (PIXELS * GROUP * HALF * 4)) + EPS)
         mean, inv = wide(mean), wide(inv)
         stats[k, 0:1, :] = mean.reshape(1, C)
         stats[k, 1:2, :] = inv.reshape(1, C)
@@ -596,10 +629,9 @@
             weight_copy(k).wait()
 
         wait_all(k, recv_a)
-        swap_cores(k, chips_moments(k))
+        swap_cores(buf_b, k, chips_moments(k), send_b, recv_b)
         for copy in ring_copies(k):
             copy.wait_recv()
-        core_copy(k).wait_recv()
         mean, inv = finish_moments(k)
 
         @pl.when(k < 5)
@@ -620,12 +652,24 @@
     lax.fori_loop(0, 6, forward, 0)
     slope(5, T - 1, T + H + 1)
 
+    def drain_sums(t):
+        wait_all(t, send_a)
+        core_copy(buf_b, t, send_b, recv_b).wait_send()
+        core_copy(pair, t, send_p, recv_p).wait_send()
+
     def drain(k, carry):
-        wait_all(k, send_a)
-        core_copy(k).wait_send()
+        drain_sums(k)
         for copy in ring_copies(k) + wide_copies(k):
             copy.wait_send()
         return carry
+
+    def drain_layer(l):
+        drain_sums(8 - l)
+        phase_wait(cor_a.at[l], csend.at[l])
+        phase_wait(cor_b.at[l], csend.at[l + 3])
+        phase_wait(cor_c.at[l], csend.at[l + 6])
+        for copy in grad_copies(l, l == 0):
+            copy.wait_send()
 
     def layer(l, last):
         k = 2 * l
@@ -646,10 +690,14 @@
         d = tap_conv_back(k, H, W) * slopes[k, T - 1 : T - 1 + H, 0:W]
         put_sums(4, d, normed(k, tile_rows, tile_columns))
         pack_sums(t)
-        send_all(t, grad_copies(l, last), [])
+        send_all(t, join_means(swapped(pair, t, send_p, recv_p)), grad_copies(l, last))
 
         if last:
             expand(l)
+            drain_layer(2)
+            drain_layer(1)
+            for copy in fine_copies():
+                copy.wait_send()
         else:
 
             @pl.when(l == 2)
@@ -664,7 +712,8 @@
                 lax.fori_loop(0, 6, drain, 0)
 
         wait_all(t, recv_a)
-        swap_cores(t, jnp.sum(buf_a[t], axis=0, keepdims=True) * (1.0 / CHIPS))
+        half = jnp.sum(buf_a[t], axis=0, keepdims=True) * (1.0 / HALF)
+        swap_cores(buf_b, t, half, send_b, recv_b)
         if not last:
 
             @pl.when(l == 2)
@@ -676,8 +725,7 @@
         far = 1 if last else 3
         grads[l, T - far : T, tile_columns, :] = grads_in[l, 0, 3 - far : 3].astype(F32)
         grads[l, T + H : T + H + far, tile_columns, :] = grads_in[l, 1, 0:far].astype(F32)
-        core_copy(t).wait_recv()
-        sums = unpacked((buf_b[t, 0, 0:1] + buf_b[t, 1, 0:1]) * 0.5)
+        sums = unpacked(join_means(swapped(buf_b, t, send_b, recv_b)))
         first2, second2, first1_raw, second1_raw = (wide(sums[i : i + 2]) for i in (0, 2, 4, 6))
         def second_sums():
             scaled = inv2 * second2
@@ -724,16 +772,7 @@
     lax.fori_loop(0, 2, backward, 0)
     layer(0, True)
 
-    for l in range(3):
-        wait_all(8 - l, send_a)
-        core_copy(8 - l).wait_send()
-        phase_wait(cor_a.at[l], csend.at[l])
-        phase_wait(cor_b.at[l], csend.at[l + 3])
-        phase_wait(cor_c.at[l], csend.at[l + 6])
-        for copy in grad_copies(l, l == 0):
-            copy.wait_send()
-    for copy in fine_copies():
-        copy.wait_send()
+    drain_layer(0)
 
 
 def per_device(latent, cotangent, pixel_mask, res_kernels, up_kernel):
@@ -764,8 +803,10 @@
             pltpu.VMEM((H + 2, W, 3 * C), BF16),
             pltpu.VMEM((H + 1, W, 3 * C), BF16),
             pltpu.VMEM((H, W, 3 * C), BF16),
-            pltpu.VMEM((9, CHIPS, 128), F32),
+            pltpu.VMEM((9, HALF, 128), F32),
             pltpu.VMEM((9, 2, 8, 128), F32),
+            pltpu.VMEM((9, 2, 8, 128), F32),
+            pltpu.VMEM((9, 8, 128), F32),
             pltpu.VMEM((8, 128), F32),
             pltpu.VMEM((6, 8, C), F32),
             pltpu.VMEM((3, SIDE, 2, 128), F32),
@@ -774,6 +815,8 @@
             pltpu.VMEM((3, SIDE, 2, 128), F32),
             pltpu.VMEM((32, 128), F32),
             pltpu.VMEM((2, 2 * C, 2 * C), BF16),
+            dma((9,)),
+            dma((9,)),
             dma((9,)),
             dma((9,)),
             dma((9,)),

time: 115 us -> 121 us (1.052)
  Pallas kernels: 113 us -> 119 us
    pallas_call x1, Pallas kernels: 113 us -> 119 us  [per_device(): pl.pallas_call(kernel, out_shape=jax.ShapeDtypeStruct((H, W, C), F32), in...]
where the time goes in v6:
time: 121 us; the launch traced here: 120 us
  Pallas kernels  119 us (98%)
  local copies, waits for them, and re-layouts  1.87 us (2%)
    pallas_call x1, Pallas kernels, per_device(): pl.pallas_call(kernel, out_shape=jax.ShapeDtypeStruct((H, W, C), F32), in...  119 us

profile of v6, /device:TPU:1, one launch (start us, length us, event | category | flops | bytes accessed | tf_op | source)
XLA Modules:
  0.0 120.5 jit_solution(9097611924925955438)
XLA Ops:
  0.0 118.6 %shard_map.55 = f32[8,64,256]{2,1,0:T(8,128)} custom-call(s32[16,128]{1,0:T(8,128)} %mask.1, bf16[8,64,256]{2,1,0:T(8,128)(2,1)} %latent_hbm.1, bf16[16,128,256]{2,1,0:T(8,128)(2,1)} %cot_hbm.1, bf16[6,9,256,256]{3,2,1,0:T(8,128)(2,1)} %bitcast.2, bf16[9,256,256]{2,1,0:T(8,128)(2,1)} %bitcast.3), custom_call_target="tpu_custom_call" | custom-call | tf_op jit(solution)/shard_map/pallas_call | solution.py:782
  118.6 1.9 %copy.7 = f32[8,64,256]{2,1,0:T(8,128)} copy(f32[8,64,256]{2,1,0:T(8,128)} %shard_map.55) | data formatting | bytes 1048576

commit v7 on v5

--- a/solution.py
+++ b/solution.py
@@ -61,7 +61,7 @@
     return c - core + (core + 1) % 2, r
 
 
-def chip_peers(visit):
+def chip_peers(visit, middle=None):
     c, r, core, x, y = position()
     plane = [(0, c, r)] + plane_peers()[::-1]
 
@@ -72,7 +72,10 @@
             visit(dz * SIDE + slot, col, row)
         return carry
 
-    lax.fori_loop(0, 7, level, 0)
+    lax.fori_loop(0, 4, level, 0)
+    if middle is not None:
+        middle()
+    lax.fori_loop(4, 7, level, 0)
 
 
 def neighbours():
@@ -191,7 +194,7 @@
         pl.semaphore_signal(barrier, inc=1, device_id={"cols": col, "rows": row}, device_id_type=MESH)
 
     chip_peers(greet)
-    greeted = plane + column + [(0,) + p[2:] for p in neighbours()]
+    greeted = plane + [p for p in column if p[0] % 2 == 1] + [(0,) + p[2:] for p in neighbours()]
     for peer in greeted:
         greet(*peer)
 
@@ -246,7 +249,7 @@
             rows = rows + lane_swap(rows, step)
         buf_a[t, 0:1, :] = packed(rows * (1.0 / GROUP))
 
-    def send_all(t, first, then):
+    def send_all(t, first, then, middle=None):
         def send(slot, col, row):
             pltpu.make_async_remote_copy(
                 src_ref=buf_a.at[t, pl.ds(0, 1)],
@@ -257,7 +260,7 @@
                 device_id_type=MESH,
             ).start()
 
-        chip_peers(send)
+        chip_peers(send, middle)
         for copy in first:
             copy.start()
         for peer in plane:
@@ -627,6 +630,15 @@
             copy.wait_send()
         return carry
 
+    def drain_layer(l):
+        wait_all(8 - l, send_a)
+        core_copy(8 - l).wait_send()
+        phase_wait(cor_a.at[l], csend.at[l])
+        phase_wait(cor_b.at[l], csend.at[l + 3])
+        phase_wait(cor_c.at[l], csend.at[l + 6])
+        for copy in grad_copies(l, l == 0):
+            copy.wait_send()
+
     def layer(l, last):
         k = 2 * l
         mean1, inv1 = load_stats(k)
@@ -646,17 +658,27 @@
         d = tap_conv_back(k, H, W) * slopes[k, T - 1 : T - 1 + H, 0:W]
         put_sums(4, d, normed(k, tile_rows, tile_columns))
         pack_sums(t)
-        send_all(t, grad_copies(l, last), [])
-
-        if last:
-            expand(l)
-        else:
-
+
+        def middle():
             @pl.when(l == 2)
             def _():
                 correlate_b(l)
+
+        send_all(t, grad_copies(l, last), [], None if last else middle)
+
+        if last:
+            expand(l)
+            drain_layer(2)
+            drain_layer(1)
+            for copy in fine_copies():
+                copy.wait_send()
+        else:
+
+            @pl.when(l == 2)
+            def _():
                 for copy in wide_copies(5):
                     copy.wait_recv()
+                correlate_c(l)
 
             @pl.when(l == 1)
             def _():
@@ -665,12 +687,6 @@
 
         wait_all(t, recv_a)
         swap_cores(t, jnp.sum(buf_a[t], axis=0, keepdims=True) * (1.0 / CHIPS))
-        if not last:
-
-            @pl.when(l == 2)
-            def _():
-                correlate_c(l)
-
         for copy in grad_copies(l, last):
             copy.wait_recv()
         far = 1 if last else 3
@@ -724,16 +740,7 @@
     lax.fori_loop(0, 2, backward, 0)
     layer(0, True)
 
-    for l in range(3):
-        wait_all(8 - l, send_a)
-        core_copy(8 - l).wait_send()
-        phase_wait(cor_a.at[l], csend.at[l])
-        phase_wait(cor_b.at[l], csend.at[l + 3])
-        phase_wait(cor_c.at[l], csend.at[l + 6])
-        for copy in grad_copies(l, l == 0):
-            copy.wait_send()
-    for copy in fine_copies():
-        copy.wait_send()
+    drain_layer(0)
 
 
 def per_device(latent, cotangent, pixel_mask, res_kernels, up_kernel):

time: 115 us -> 112 us (0.974)
  Pallas kernels: 113 us -> 110 us
    pallas_call x1, Pallas kernels: 113 us -> 110 us  [per_device(): pl.pallas_call(kernel, out_shape=jax.ShapeDtypeStruct((H, W, C), F32), in...]
where the time goes in v7:
time: 112 us
  Pallas kernels  110 us (98%)
  local copies, waits for them, and re-layouts  1.87 us (2%)
    pallas_call x1, Pallas kernels, per_device(): pl.pallas_call(kernel, out_shape=jax.ShapeDtypeStruct((H, W, C), F32), in...  110 us

profile of v7, /device:TPU:1, one launch (start us, length us, event | category | flops | bytes accessed | tf_op | source)
XLA Modules:
  0.0 111.7 jit_solution(1595110319684674834)
XLA Ops:
  0.0 109.9 %shard_map.55 = f32[8,64,256]{2,1,0:T(8,128)} custom-call(s32[16,128]{1,0:T(8,128)} %mask.1, bf16[8,64,256]{2,1,0:T(8,128)(2,1)} %latent_hbm.1, bf16[16,128,256]{2,1,0:T(8,128)(2,1)} %cot_hbm.1, bf16[6,9,256,256]{3,2,1,0:T(8,128)(2,1)} %bitcast.2, bf16[9,256,256]{2,1,0:T(8,128)(2,1)} %bitcast.3), custom_call_target="tpu_custom_call" | custom-call | tf_op jit(solution)/shard_map/pallas_call | solution.py:750
  109.9 1.9 %copy.7 = f32[8,64,256]{2,1,0:T(8,128)} copy(f32[8,64,256]{2,1,0:T(8,128)} %shard_map.55) | data formatting | bytes 1048576

commit v8 on v7

--- a/solution.py
+++ b/solution.py
@@ -166,8 +166,8 @@
 
 
 def kernel(
-    mask, latent_hbm, cot_hbm, res_hbm, up_hbm, out,
-    latent, cot, weights, fields, grads, grads_out, grads_in, total, pre, fine, rows_out, rows_in, slopes, stats, taps, taps_n, box_a, box_b,
+    mask_hbm, latent_hbm, cot_hbm, res_hbm, up_hbm, out_hbm,
+    mask, out, latent, cot, weights, fields, grads, grads_out, grads_in, total, pre, fine, rows_out, rows_in, slopes, stats, taps, taps_n, box_a, box_b,
     buf_a, buf_b, lines, means, cor_own, cor_a, cor_b, cor_c, cor, expanded,
     load_sem, send_a, send_b, recv_a, recv_b, csend, crecv, hsend, hrecv,
 ):
@@ -185,6 +185,8 @@
 
     up_copy = pltpu.make_async_copy(up_hbm, weights.at[6], load_sem.at[6])
     cot_copy = pltpu.make_async_copy(cot_hbm, cot, load_sem.at[7])
+    mask_copy = pltpu.make_async_copy(mask_hbm, mask, load_sem.at[9])
+    out_copy = pltpu.make_async_copy(out, out_hbm, load_sem.at[10])
     latent_copy = pltpu.make_async_copy(latent_hbm, latent, load_sem.at[8])
     latent_copy.start()
     barrier = pltpu.get_barrier_semaphore()
@@ -198,6 +200,7 @@
     for peer in greeted:
         greet(*peer)
 
+    mask_copy.start()
     cot_copy.start()
     weight_copy(0).start()
     up_copy.start()
@@ -385,6 +388,7 @@
 
     pl.semaphore_wait(barrier, CHIPS - SIDE + len(greeted))
     send_all(0, ring_copies(0), wide_copies(0))
+    mask_copy.wait()
     cot_copy.wait()
 
     def mask_row(i, carry):
@@ -740,19 +744,22 @@
     lax.fori_loop(0, 2, backward, 0)
     layer(0, True)
 
+    out_copy.start()
     drain_layer(0)
+    out_copy.wait()
 
 
 def per_device(latent, cotangent, pixel_mask, res_kernels, up_kernel):
-    vmem = pl.BlockSpec(memory_space=pltpu.VMEM)
     hbm = pl.BlockSpec(memory_space=pl.ANY)
     dma = pltpu.SemaphoreType.DMA
     return pl.pallas_call(
         kernel,
         out_shape=jax.ShapeDtypeStruct((H, W, C), F32),
-        in_specs=[vmem, hbm, hbm, hbm, hbm],
-        out_specs=vmem,
+        in_specs=[hbm, hbm, hbm, hbm, hbm],
+        out_specs=hbm,
         scratch_shapes=[
+            pltpu.VMEM((FH, FW), jnp.int32),
+            pltpu.VMEM((H, W, C), F32),
             pltpu.VMEM((H, W, C), BF16),
             pltpu.VMEM((FH, FW, C), BF16),
             pltpu.VMEM((7, 9, C, C), BF16),
@@ -781,7 +788,7 @@
             pltpu.VMEM((3, SIDE, 2, 128), F32),
             pltpu.VMEM((32, 128), F32),
             pltpu.VMEM((2, 2 * C, 2 * C), BF16),
-            dma((9,)),
+            dma((11,)),
             dma((9,)),
             dma((9,)),
             dma((9,)),

time: 112 us -> 112 us (level)
  no operation moved by 1% of the time
where the time goes in v8:
time: 112 us
  Pallas kernels  110 us (98%)
  local copies, waits for them, and re-layouts  1.87 us (2%)
    pallas_call x1, Pallas kernels, per_device(): pl.pallas_call(kernel, out_shape=jax.ShapeDtypeStruct((H, W, C), F32), in...  110 us

profile of v8, /device:TPU:1, one launch (start us, length us, event | category | flops | bytes accessed | tf_op | source)
XLA Modules:
  0.0 111.5 jit_solution(9447574261592377644)
XLA Ops:
  0.0 109.6 %shard_map.55 = f32[8,64,256]{2,1,0:T(8,128)} custom-call(s32[16,128]{1,0:T(8,128)} %mask_hbm.1, bf16[8,64,256]{2,1,0:T(8,128)(2,1)} %latent_hbm.1, bf16[16,128,256]{2,1,0:T(8,128)(2,1)} %cot_hbm.1, bf16[6,9,256,256]{3,2,1,0:T(8,128)(2,1)} %bitcast.2, bf16[9,256,256]{2,1,0:T(8,128)(2,1)} %bitcast.3), custom_call_target="tpu_custom_call" | custom-call | tf_op jit(solution)/shard_map/pallas_call | solution.py:755
  109.6 1.9 %copy.7 = f32[8,64,256]{2,1,0:T(8,128)} copy(f32[8,64,256]{2,1,0:T(8,128)} %shard_map.55) | data formatting | bytes 1048576
